TPU v7x, 32 devices: a whole 2x2x4 slice. The times are simulated.
32 devices in a mesh: grp: 2 (over y), reg: 16 (over z, x, core).
Axes of the slice: x: 2, y: 2, z: 4, core: 2. Of those that a mesh axis runs over, the one named last changes fastest.
Arguments:
- obs_value: float32 [512, 128, 256], P(('grp', 'reg')), parts along dimension 0, may hold values from -12 to 12
- positions: float32 [2, 512, 256], P(None, ('grp', 'reg')), parts along dimension 1, may hold values from 0 to 25
- sigma: float32 [512, 256], P(('grp', 'reg')), parts along dimension 0, may hold values from 0.5 to 2
- obs_var: float32 [512, 256], P(('grp', 'reg')), parts along dimension 0, may hold values from 0.3 to 3
- class_amp: float32 [3, 3], replicated, may hold values from 0.2 to 1
- length_scale: float32 [3], replicated, may hold values from 0.09 to 0.19
- block_class: int32 [512], P(('grp', 'reg')), parts along dimension 0, may hold values from 0 to 2
- block_count: int32 [32], P(('grp', 'reg')), parts along dimension 0, may hold values from 6 to 16, as said below
- pair_list: int32 [2, 1952], P(None, ('grp', 'reg')), parts along dimension 1, may hold values from 0 to 15, as said below
- pair_count: int32 [2, 32], P(None, ('grp', 'reg')), parts along dimension 1, may hold values from 0 to 46, as said below
Outputs:
- analysis_weights: float32 [512, 128, 256], P(('grp', 'reg')), parts along dimension 0
- residual: float32 [512, 128, 256], P(('grp', 'reg')), parts along dimension 0
There are 2 independent parts, one for each index of `grp`. A program takes and returns all parts, laid end to end along the dimension named above; an argument that names none is the same for every part. Nothing has to cross between parts.
Inputs may be any that keep to these rules, and one draw needn't show every extreme that they name: `block_count`: A region's live blocks are its slots below its count; in every draw two neighbouring regions hold 16 live blocks. `pair_list`: listed pairs join live blocks only, each block pair at most once; within a region's 61 entries the pairs inside the region come first, then those with the next region, then unused entries. Some region fills all 61 entries in every draw. pair_count[0, r] + pair_count[1, r] <= 61; the last region has no pairs with a next region.
All inputs are finite; a program needn't handle non-finite values.
Results may differ from a plain program's by a relative error of at most 0.0003.
Values sent between devices are 32-bit elements; how exact they have to be, the bound alone decides.
A program may use at most 64 MiB of HBM per device.

v0:
```python
import jax
import jax.numpy as jnp
from jax import lax
from jax.sharding import PartitionSpec as P

ITERS = 2


highest_precision = lax.Precision.HIGHEST


def passed_along(shard, axis, by):
    length = lax.axis_size(axis)
    pairs = [(i, i + by) for i in range(length) if 0 <= i + by < length]
    return lax.ppermute(shard, axis, pairs)


def gaspari(ratio):
    inner = (((-0.25 * ratio + 0.5) * ratio + 0.625) * ratio - 5.0 / 3.0) * ratio * ratio + 1.0
    safe_ratio = jnp.maximum(ratio, 1.0)
    outer = (
        ((((ratio / 12.0 - 0.5) * ratio + 0.625) * ratio + 5.0 / 3.0) * ratio - 5.0) * ratio
        + 4.0
        - 2.0 / (3.0 * safe_ratio)
    )
    return jnp.where(ratio <= 1.0, inner, jnp.where(ratio <= 2.0, outer, jnp.zeros_like(ratio)))


def amplitude_rows(block_class, class_amp):
    class_ids = jnp.arange(class_amp.shape[0], dtype=jnp.int32)
    chosen = block_class[:, None, None] == class_ids[None, :, None]
    return jnp.sum(
        jnp.where(chosen, class_amp[None, :, :], jnp.zeros_like(class_amp)[None]), axis=1
    )


def corr_tile(pos_first, pos_second, amp_first, amp_second, length_scale):
    east_gap = pos_first[0][:, None] - pos_second[0][None, :]
    north_gap = pos_first[1][:, None] - pos_second[1][None, :]
    distance = jnp.sqrt(east_gap * east_gap + north_gap * north_gap)
    running = jnp.zeros_like(distance)
    for cls_index in range(length_scale.shape[0]):
        running = running + amp_first[cls_index] * amp_second[cls_index] * gaspari(
            distance / length_scale[cls_index]
        )
    return running


def build_tiles(pos_first, pos_second, amp_first, amp_second, length_scale):
    return jax.vmap(corr_tile, in_axes=(1, 1, 0, 0, None))(
        pos_first, pos_second, amp_first, amp_second, length_scale
    )


def pair_tiles_of(pos_all, amp_all, first_rows, second_rows, length_scale):
    return build_tiles(
        pos_all[:, first_rows],
        pos_all[:, second_rows],
        amp_all[first_rows],
        amp_all[second_rows],
        length_scale,
    )


def selector(rows, count):
    return (rows[:, None] == jnp.arange(count, dtype=jnp.int32)[None, :]).astype(jnp.float32)


def pick_rows(select, values):
    return jnp.einsum("ts,smq->tmq", select, values, precision=highest_precision)


def place_rows(select, terms):
    return jnp.einsum("ts,tmp->smp", select, terms, precision=highest_precision)


def apply_forward(tiles, values, weight):
    return (
        jnp.einsum("tpq,tmq->tmp", tiles, values, precision=highest_precision)
        * weight[:, None, None]
    )


def apply_backward(tiles, values, weight):
    return (
        jnp.einsum("tpq,tmp->tmq", tiles, values, precision=highest_precision)
        * weight[:, None, None]
    )


def local(
    obs_value,
    positions,
    sigma,
    obs_var,
    class_amp,
    length_scale,
    block_class,
    block_count,
    pair_list,
    pair_count,
):
    block_slots = obs_value.shape[0]
    entry_total = pair_list.shape[1]
    amp_rows = amplitude_rows(block_class, class_amp)
    slot_ids = jnp.arange(block_slots, dtype=jnp.int32)
    entry_ids = jnp.arange(entry_total, dtype=jnp.int32)
    live_mask = (slot_ids < block_count[0]).astype(jnp.float32)
    local_pairs = pair_count[0, 0]
    cross_pairs = pair_count[1, 0]
    in_listed = (entry_ids < local_pairs + cross_pairs).astype(jnp.float32)
    cross_offset = jnp.where(entry_ids >= local_pairs, block_slots, 0).astype(jnp.int32)
    north_pos, north_amp = passed_along((positions, amp_rows), "reg", -1)
    diag_tiles = build_tiles(positions, positions, amp_rows, amp_rows, length_scale)
    pos_two = jnp.concatenate([positions, north_pos], axis=1)
    amp_two = jnp.concatenate([amp_rows, north_amp], axis=0)
    pair_first = pair_list[0]
    pair_second = pair_list[1] + cross_offset
    pair_tiles = pair_tiles_of(pos_two, amp_two, pair_first, pair_second, length_scale)
    first_sel = selector(pair_first, 2 * block_slots)
    second_sel = selector(pair_second, 2 * block_slots)

    def squares(vector):
        return lax.psum(jnp.sum(vector * vector, axis=(0, 2)), "reg")

    residual = obs_value * live_mask[:, None, None]
    weights = jnp.zeros_like(residual)
    direction = residual
    norm_now = squares(residual)
    for iteration in range(ITERS):
        scaled = sigma[:, None, :] * direction
        diag_terms = jnp.einsum("bpq,bmq->bmp", diag_tiles, scaled, precision=highest_precision)
        north_vals = passed_along(scaled, "reg", -1)
        values_two = jnp.concatenate([scaled, north_vals], axis=0)
        forward_terms = apply_forward(pair_tiles, pick_rows(second_sel, values_two), in_listed)
        backward_terms = apply_backward(pair_tiles, pick_rows(first_sel, values_two), in_listed)
        collected = place_rows(first_sel, forward_terms) + place_rows(second_sel, backward_terms)
        returned = passed_along(collected[block_slots:], "reg", 1)
        spread = diag_terms + collected[:block_slots] + returned
        applied = sigma[:, None, :] * spread + obs_var[:, None, :] * direction
        curvature = lax.psum(jnp.sum(direction * applied, axis=(0, 2)), "reg")
        step_size = norm_now / curvature
        weights = weights + step_size[None, :, None] * direction
        residual = residual - step_size[None, :, None] * applied
        if iteration + 1 < ITERS:
            norm_next = squares(residual)
            direction = residual + (norm_next / norm_now)[None, :, None] * direction
            norm_now = norm_next
    return (weights, residual)


def solution(mesh):
    placed = (
        P(("grp", "reg"), None, None),
        P(None, ("grp", "reg"), None),
        P(("grp", "reg"), None),
        P(("grp", "reg"), None),
        P(),
        P(),
        P(("grp", "reg")),
        P(("grp", "reg")),
        P(None, ("grp", "reg")),
        P(None, ("grp", "reg")),
    )
    return jax.shard_map(
        local,
        mesh=mesh,
        in_specs=placed,
        out_specs=(P(("grp", "reg"), None, None), P(("grp", "reg"), None, None)),
        check_vma=False,
    )
```

profile of v0, /device:TPU:0, one launch (start us, length us, event | category | flops | bytes accessed | tf_op | source)
XLA Modules:
  0.0 666.9 jit_solution(12929422196349293960)
XLA Ops:
  0.6 0.7 iota_compare_fusion.2
  1.3 0.8 select_reduce_fusion
  2.1 1.3 collective-permute-start.1
  4.0 1.9 multiply_multiply_fusion.6
  6.0 1.3 collective-permute-start
  7.3 0.8 fusion.191
  8.1 1.3 collective-permute-start.2
  9.4 1.3 fusion.193
  12.0 1.4 fusion.192
  13.4 1.4 fusion.109
  14.8 0.7 slice_bitcast_fusion.2
  15.5 1.3 fusion.107
  16.8 0.0 collective-permute-done.1
  16.8 0.1 pad_maximum_fusion.2
  16.9 0.1 copy.43
  17.0 0.6 gather_fusion.1
  17.6 0.6 gather_fusion
  18.2 0.2 fusion.88
  18.4 0.0 collective-permute-done.2
  18.4 0.7 gather_fusion.3
  19.1 0.7 gather_fusion.2
  19.8 0.1 fusion.190
  19.9 0.1 fusion.189
  20.1 1.9 pad_maximum_fusion
  22.0 6.3 fusion.52
  28.4 7.8 %fusion.54 = f32[61,128,256]{2,0,1:T(8,128)} fusion(f32[32,128,256]{2,1,0:T(8,128)S(1)} %pad_maximum_fusion, s32[61]{0:T(128)S(1)} %fusion.107), kind=kOutput, calls=%fused_computation.70 | convolution fusion | flops 767559552 | bytes 12189940 | tf_op jit(solution)/shard_map/ts,smq->tmq/dot_general | solution.py:70
  36.2 80.0 %broadcast_multiply_fusion.2 = f32[61,128,256]{2,1,0:T(8,128)S(1)} fusion(f32[61]{0:T(128)S(1)} %compare_convert_fusion, f32[]{:T(128)} %bitcast.8, f32[61]{0:T(128)S(1)} %get-tuple-element.6, f32[]{:T(128)} %bitcast.6, f32[61]{0:T(128)S(1)} %get-tuple-element.5, f32[]{:T(128)} %bitcast.4, f32[61,256]{1,0:T(8,128)S(1)} %bitcast.71, ...), kind=kOutput, calls=%fused_computation.62 | convolution fusion | flops 6518243328 | bytes 16241628 | tf_op jit(solution)/shard_map/tpq,tmp->tmq/dot_general | solution.py:86
  116.2 7.8 %fusion.18 = f32[32,128,256]{2,0,1:T(8,128)} fusion(f32[61,128,256]{2,1,0:T(8,128)S(1)} %broadcast_multiply_fusion.2, s32[61]{0:T(128)S(1)} %copy-done.23), kind=kOutput, calls=%fused_computation.26 | convolution fusion | flops 767559552 | bytes 12189940 | tf_op jit(solution)/shard_map/ts,tmp->smp/dot_general | solution.py:74
  124.0 83.9 %broadcast_multiply_fusion.3 = f32[61,128,256]{2,1,0:T(8,128)S(1)} fusion(f32[61]{0:T(128)S(1)} %compare_convert_fusion, f32[]{:T(128)} %bitcast.8, f32[61]{0:T(128)S(1)} %get-tuple-element.6, f32[]{:T(128)} %bitcast.6, f32[61]{0:T(128)S(1)} %get-tuple-element.5, f32[]{:T(128)} %bitcast.4, f32[61,256]{1,0:T(8,128)S(1)} %bitcast.72, ...), kind=kOutput, calls=%fused_computation.63 | convolution fusion | flops 6518243328 | bytes 16241628 | tf_op jit(solution)/shard_map/tpq,tmq->tmp/dot_general | solution.py:79
  207.9 8.0 %fusion.20 = f32[32,128,256]{2,0,1:T(8,128)S(1)} fusion(f32[61,128,256]{2,1,0:T(8,128)S(1)} %broadcast_multiply_fusion.3, s32[61]{0:T(128)S(1)} %copy-done.20), kind=kOutput, calls=%fused_computation.28 | convolution fusion | flops 767559552 | bytes 12189940 | tf_op jit(solution)/shard_map/ts,tmp->smp/dot_general | solution.py:74
  215.9 0.0 copy-start.15
  216.0 0.0 copy-start.7
  216.0 0.0 copy-start
  216.0 0.0 copy-start.8
  216.0 0.0 copy-start.34
  216.0 4.8 copy_add_fusion.1
  220.8 0.1 slice.131
  220.9 19.3 %collective-permute-start.3 = (f32[16,128,256]{2,1,0:T(8,128)S(1)}, f32[16,128,256]{2,1,0:T(8,128)S(1)}, u32[]{:S(2)}, u32[]{:S(2)}) collective-permute-start(f32[16,128,256]{2,1,0:T(8,128)S(1)} %slice.131), channel_id=1, source_target_pairs={{0,1},{1,2},{2,3},{3,4},{4,5},{5,6},{6,7},{7,8},{8,9},{9,10},{10,1... | collective-permute-start | bytes 6291464 | tf_op jit(solution)/shard_map/ppermute | solution.py:15
  240.3 3.5 collective-permute-done.3
  243.9 25.3 %multiply_reduce_fusion.2 = (f32[128]{0:T(128)S(1)}, f32[128]{0:T(128)S(1)}, f32[16,128,256]{2,1,0:T(8,128)}) fusion(f32[16,128,256]{2,1,0:T(8,128)S(1)} %copy-done, f32[16]{0:T(128)S(1)} %copy-done.17, f32[16,256]{1,0:T(8,128)S(1)} %copy-done.34, f32[16,128,256]{2,1,0:T(8,128)S(1)} %collective-permute-done.3, f32[32,128,256]{2,1,0:T(8,128)S(1)} %copy_add_fusion.1, ...), kind=kOutput, calls=%fused_computation.86 | convolution fusion | flops 1715470080 | bytes 10604044 | tf_op jit(solution)/shard_map/bpq,bmq->bmp/dot_general | solution.py:132
  269.2 49.9 %all-reduce = (f32[128]{0:T(128)S(1)}, f32[128]{0:T(128)S(1)}) all-reduce(f32[128]{0:T(128)S(1)} %get-tuple-element.3, f32[128]{0:T(128)S(1)} %get-tuple-element.2), channel_id=1, replica_groups=mesh['grp'=2,'reg'=16] {'reg'}, use_global_device_ids=true, to_apply=%region_1.2 | all-reduce | flops 256 | bytes 2048 | tf_op jit(solution)/shard_map/psum | solution.py:124
  319.2 2.1 multiply_reduce_fusion.1
  321.2 29.8 %psum.30 = f32[128]{0:T(128)S(1)} all-reduce(f32[128]{0:T(128)S(1)} %multiply_reduce_fusion.1), channel_id=1, replica_groups=mesh['grp'=2,'reg'=16] {'reg'}, use_global_device_ids=true, to_apply=%region_6.7 | all-reduce | flops 128 | bytes 1024 | tf_op jit(solution)/shard_map/psum | solution.py:124
  351.1 3.5 broadcast_multiply_fusion.4
  354.6 1.3 collective-permute-start.4
  355.9 4.8 collective-permute-done.4
  360.6 0.4 pad_maximum_fusion.1
  361.0 6.3 fusion.48
  367.3 7.8 %fusion.50 = f32[61,128,256]{2,0,1:T(8,128)} fusion(f32[32,128,256]{2,1,0:T(8,128)S(1)} %pad_maximum_fusion.1, s32[61]{0:T(128)S(1)} %copy-done.24), kind=kOutput, calls=%fused_computation.66 | convolution fusion | flops 767559552 | bytes 12189940 | tf_op jit(solution)/shard_map/ts,smq->tmq/dot_general | solution.py:70
  375.2 80.0 %broadcast_multiply_fusion = f32[61,128,256]{2,1,0:T(8,128)S(1)} fusion(f32[61]{0:T(128)S(1)} %compare_convert_fusion, f32[]{:T(128)} %bitcast.8, f32[61]{0:T(128)S(1)} %get-tuple-element.6, f32[]{:T(128)} %bitcast.6, f32[61]{0:T(128)S(1)} %get-tuple-element.5, f32[]{:T(128)} %bitcast.4, f32[61,256]{1,0:T(8,128)S(1)} %bitcast.73, ...), kind=kOutput, calls=%fused_computation.60 | convolution fusion | flops 6518243328 | bytes 16241628 | tf_op jit(solution)/shard_map/tpq,tmp->tmq/dot_general | solution.py:86
  455.2 7.8 %fusion.14 = f32[32,128,256]{2,0,1:T(8,128)} fusion(f32[61,128,256]{2,1,0:T(8,128)S(1)} %broadcast_multiply_fusion, s32[61]{0:T(128)S(1)} %copy-done.25), kind=kOutput, calls=%fused_computation.22 | convolution fusion | flops 767559552 | bytes 12189940 | tf_op jit(solution)/shard_map/ts,tmp->smp/dot_general | solution.py:74
  463.0 83.8 %broadcast_multiply_fusion.1 = f32[61,128,256]{2,1,0:T(8,128)S(1)} fusion(f32[61]{0:T(128)S(1)} %compare_convert_fusion, f32[]{:T(128)} %bitcast.8, f32[61]{0:T(128)S(1)} %get-tuple-element.6, f32[]{:T(128)} %bitcast.6, f32[61]{0:T(128)S(1)} %get-tuple-element.5, f32[]{:T(128)} %bitcast.4, f32[61,256]{1,0:T(8,128)S(1)} %bitcast.74, ...), kind=kOutput, calls=%fused_computation.61 | convolution fusion | flops 6518243328 | bytes 16241628 | tf_op jit(solution)/shard_map/tpq,tmq->tmp/dot_general | solution.py:79
  546.8 8.0 %fusion.16 = f32[32,128,256]{2,0,1:T(8,128)S(1)} fusion(f32[61,128,256]{2,1,0:T(8,128)S(1)} %broadcast_multiply_fusion.1, s32[61]{0:T(128)S(1)} %copy-done.21), kind=kOutput, calls=%fused_computation.24 | convolution fusion | flops 767559552 | bytes 12189940 | tf_op jit(solution)/shard_map/ts,tmp->smp/dot_general | solution.py:74
  554.8 0.0 copy-start.4
  554.8 0.0 copy-start.9
  554.9 0.0 copy-start.35
  554.9 4.9 copy_add_fusion
  559.8 0.1 slice.133
  559.9 22.9 %collective-permute-start.5 = (f32[16,128,256]{2,1,0:T(8,128)S(1)}, f32[16,128,256]{2,1,0:T(8,128)S(1)}, u32[]{:S(2)}, u32[]{:S(2)}) collective-permute-start(f32[16,128,256]{2,1,0:T(8,128)S(1)} %slice.133), channel_id=1, source_target_pairs={{0,1},{1,2},{2,3},{3,4},{4,5},{5,6},{6,7},{7,8},{8,9},{9,10},{10,1... | collective-permute-start | bytes 6291464 | tf_op jit(solution)/shard_map/ppermute | solution.py:15
  582.8 3.6 collective-permute-done.5
  586.5 0.0 copy-start.1
  586.5 25.2 %multiply_reduce_fusion = (f32[128]{0:T(128)S(1)}, f32[16,128,256]{2,1,0:T(8,128)}) fusion(f32[16,128,256]{2,1,0:T(8,128)S(1)} %copy-done.4, f32[16,256]{1,0:T(8,128)S(1)} %copy-done.35, f32[16,128,256]{2,1,0:T(8,128)S(1)} %collective-permute-done.5, f32[32,128,256]{2,1,0:T(8,128)S(1)} %copy_add_fusion, f32[]{:T(128)} %bitcast.8, f32[16]{0:T(128)S(1)} %copy-done.31, ...), kind=kOutput, calls=%fused_computation.82 | convolution fusion | flops 1713373056 | bytes 10602508 | tf_op jit(solution)/shard_map/bpq,bmq->bmp/dot_general | solution.py:132
  611.7 48.7 %psum.31 = f32[128]{0:T(128)S(1)} all-reduce(f32[128]{0:T(128)S(1)} %get-tuple-element.32), channel_id=1, replica_groups=mesh['grp'=2,'reg'=16] {'reg'}, use_global_device_ids=true, to_apply=%region_8.9 | all-reduce | flops 128 | bytes 1024 | tf_op jit(solution)/shard_map/psum | solution.py:141
  660.5 6.0 multiply_subtract_fusion
  (81 shorter events, 0.2 us)
Async XLA Ops:
  2.1 14.8 %copy-start.14 = (f32[16,3]{0,1:T(4,128)}, f32[16,3]{0,1:T(4,128)S(1)}, u32[]{:S(2)}) copy-start(f32[16,3]{0,1:T(4,128)S(1)} %select_reduce_fusion) | copy-start | bytes 580
  2.1 14.8 %collective-permute-start.1 = (f32[16,3]{0,1:T(4,128)S(1)}, f32[16,3]{0,1:T(4,128)S(1)}, u32[]{:S(2)}, u32[]{:S(2)}) collective-permute-start(f32[16,3]{0,1:T(4,128)S(1)} %select_reduce_fusion), channel_id=1, source_target_pairs={{1,0},{2,1},{3,2},{4,3},{5,4},{6,5},{7,6},{8,7},{9,8},{10,9},{11,1... | collective-permute-start | bytes 584 | tf_op jit(solution)/shard_map/ppermute | solution.py:15
  4.0 5.4 copy-start.16
  6.0 14.1 %collective-permute-start = (f32[16,128,256]{2,1,0:T(8,128)S(1)}, f32[16,128,256]{2,1,0:T(8,128)}, u32[]{:S(2)}, u32[]{:S(2)}) collective-permute-start(f32[16,128,256]{2,1,0:T(8,128)S(1)} %multiply_multiply_fusion.6), channel_id=1, source_target_pairs={{1,0},{2,1},{3,2},{4,3},{5,4},{6,5},{7,6},{8,7},{9,8},{10,9},{11,1... | collective-permute-start | bytes 6291464 | tf_op jit(solution)/shard_map/ppermute | solution.py:15
  8.1 10.3 %collective-permute-start.2 = (f32[2,16,256]{2,0,1:T(2,128)S(1)}, f32[2,16,256]{2,0,1:T(2,128)S(1)}, u32[]{:S(2)}, u32[]{:S(2)}) collective-permute-start(f32[2,16,256]{2,0,1:T(2,128)S(1)} %get-tuple-element.19), channel_id=1, source_target_pairs={{1,0},{2,1},{3,2},{4,3},{5,4},{6,5},{7,6},{8,7},{9,8},{10,9},{11,1... | collective-permute-start | bytes 98312 | tf_op jit(solution)/shard_map/ppermute | solution.py:15
  15.5 12.9 %copy-start.19 = (s32[61]{0:T(128)}, s32[61]{0:T(128)S(1)}, u32[]{:S(2)}) copy-start(s32[61]{0:T(128)S(1)} %slice_bitcast_fusion.2) | copy-start | bytes 736
  16.8 11.6 %copy-start.22 = (s32[61]{0:T(128)}, s32[61]{0:T(128)S(1)}, u32[]{:S(2)}) copy-start(s32[61]{0:T(128)S(1)} %fusion.107) | copy-start | bytes 736
  36.2 80.0 %copy-start.23 = (s32[61]{0:T(128)S(1)}, s32[61]{0:T(128)}, u32[]{:S(2)}) copy-start(s32[61]{0:T(128)} %copy-done.22) | copy-start | bytes 736
  116.2 7.8 %copy-start.6 = (f32[61,128,256]{2,0,1:T(8,128)S(1)}, f32[61,128,256]{2,0,1:T(8,128)}, u32[]{:S(2)}) copy-start(f32[61,128,256]{2,0,1:T(8,128)} %fusion.54) | copy-start | bytes 23986180
  124.0 83.9 %copy-start.20 = (s32[61]{0:T(128)S(1)}, s32[61]{0:T(128)}, u32[]{:S(2)}) copy-start(s32[61]{0:T(128)} %copy-done.19) | copy-start | bytes 736
  207.9 8.0 %copy-start.3 = (f32[32,128,256]{2,0,1:T(8,128)S(1)}, f32[32,128,256]{2,0,1:T(8,128)}, u32[]{:S(2)}) copy-start(f32[32,128,256]{2,0,1:T(8,128)} %fusion.18) | copy-start | bytes 12582916
  215.9 24.3 %copy-start.15 = (f32[16,3]{0,1:T(4,128)S(1)}, f32[16,3]{0,1:T(4,128)}, u32[]{:S(2)}) copy-start(f32[16,3]{0,1:T(4,128)} %copy-done.14) | copy-start | bytes 580
  216.0 24.3 %copy-start.7 = (f32[2,16,256]{2,1,0:T(8,128)S(1)}, f32[2,16,256]{2,1,0:T(8,128)}, u32[]{:S(2)}) copy-start(f32[2,16,256]{2,1,0:T(8,128)} %param.11) | copy-start | bytes 98308
  216.0 27.9 %copy-start = (f32[16,128,256]{2,1,0:T(8,128)S(1)}, f32[16,128,256]{2,1,0:T(8,128)}, u32[]{:S(2)}) copy-start(f32[16,128,256]{2,1,0:T(8,128)} %param.10) | copy-start | bytes 6291460
  216.0 27.9 %copy-start.8 = (f32[16,256]{1,0:T(8,128)S(1)}, f32[16,256]{1,0:T(8,128)}, u32[]{:S(2)}) copy-start(f32[16,256]{1,0:T(8,128)} %param.12) | copy-start | bytes 49156
  216.0 27.9 %copy-start.17 = (f32[16]{0:T(128)S(1)}, f32[16]{0:T(128)}, u32[]{:S(2)}) copy-start(f32[16]{0:T(128)} %copy-done.16) | copy-start | bytes 196
  216.0 27.8 %copy-start.34 = (f32[16,256]{1,0:T(8,128)S(1)}, f32[16,256]{1,0:T(8,128)}, u32[]{:S(2)}) copy-start(f32[16,256]{1,0:T(8,128)} %param.13) | copy-start | bytes 49156
  220.9 22.9 %collective-permute-start.3 = (f32[16,128,256]{2,1,0:T(8,128)S(1)}, f32[16,128,256]{2,1,0:T(8,128)S(1)}, u32[]{:S(2)}, u32[]{:S(2)}) collective-permute-start(f32[16,128,256]{2,1,0:T(8,128)S(1)} %slice.131), channel_id=1, source_target_pairs={{0,1},{1,2},{2,3},{3,4},{4,5},{5,6},{6,7},{7,8},{8,9},{9,10},{10,1... | collective-permute-start | bytes 6291464 | tf_op jit(solution)/shard_map/ppermute | solution.py:15
  240.2 28.9 %copy-start.28 = (f32[16]{0:T(128)}, f32[16]{0:T(128)S(1)}, u32[]{:S(2)}) copy-start(f32[16]{0:T(128)S(1)} %get-tuple-element.21) | copy-start | bytes 196
  240.2 28.9 %copy-start.30 = (f32[16]{0:T(128)}, f32[16]{0:T(128)S(1)}, u32[]{:S(2)}) copy-start(f32[16]{0:T(128)S(1)} %get-tuple-element.22) | copy-start | bytes 196
  240.3 28.9 %copy-start.32 = (f32[16]{0:T(128)}, f32[16]{0:T(128)S(1)}, u32[]{:S(2)}) copy-start(f32[16]{0:T(128)S(1)} %get-tuple-element.23) | copy-start | bytes 196
  240.3 28.9 %copy-start.10 = (f32[16,256]{1,0:T(8,128)}, f32[16,256]{1,0:T(8,128)S(1)}, u32[]{:S(2)}) copy-start(f32[16,256]{1,0:T(8,128)S(1)} %get-tuple-element.17) | copy-start | bytes 49156
  240.3 28.9 %copy-start.12 = (f32[16,256]{1,0:T(8,128)}, f32[16,256]{1,0:T(8,128)S(1)}, u32[]{:S(2)}) copy-start(f32[16,256]{1,0:T(8,128)S(1)} %get-tuple-element.18) | copy-start | bytes 49156
  319.2 41.5 %copy-start.26 = (f32[128]{0:T(128)}, f32[128]{0:T(128)S(1)}, u32[]{:S(2)}) copy-start(f32[128]{0:T(128)S(1)} %div.105) | copy-start | bytes 1540
  351.1 9.9 %copy-start.36 = (f32[128]{0:T(128)}, f32[128]{0:T(128)S(1)}, u32[]{:S(2)}) copy-start(f32[128]{0:T(128)S(1)} %psum.30) | copy-start | bytes 1540
  354.6 6.0 collective-permute-start.4
  361.0 6.3 copy-start.24
  375.2 80.0 %copy-start.25 = (s32[61]{0:T(128)S(1)}, s32[61]{0:T(128)}, u32[]{:S(2)}) copy-start(s32[61]{0:T(128)} %copy-done.22) | copy-start | bytes 736
  455.2 7.8 %copy-start.5 = (f32[61,128,256]{2,0,1:T(8,128)S(1)}, f32[61,128,256]{2,0,1:T(8,128)}, u32[]{:S(2)}) copy-start(f32[61,128,256]{2,0,1:T(8,128)} %fusion.50) | copy-start | bytes 23986180
  463.0 83.8 %copy-start.21 = (s32[61]{0:T(128)S(1)}, s32[61]{0:T(128)}, u32[]{:S(2)}) copy-start(s32[61]{0:T(128)} %copy-done.19) | copy-start | bytes 736
  546.8 8.0 %copy-start.2 = (f32[32,128,256]{2,0,1:T(8,128)S(1)}, f32[32,128,256]{2,0,1:T(8,128)}, u32[]{:S(2)}) copy-start(f32[32,128,256]{2,0,1:T(8,128)} %fusion.14) | copy-start | bytes 12582916
  554.8 31.6 %copy-start.4 = (f32[16,128,256]{2,1,0:T(8,128)S(1)}, f32[16,128,256]{2,1,0:T(8,128)}, u32[]{:S(2)}) copy-start(f32[16,128,256]{2,1,0:T(8,128)} %get-tuple-element.10) | copy-start | bytes 6291460
  554.8 31.6 %copy-start.9 = (f32[16,256]{1,0:T(8,128)S(1)}, f32[16,256]{1,0:T(8,128)}, u32[]{:S(2)}) copy-start(f32[16,256]{1,0:T(8,128)} %param.12) | copy-start | bytes 49156
  554.8 31.6 %copy-start.11 = (f32[16,256]{1,0:T(8,128)S(1)}, f32[16,256]{1,0:T(8,128)}, u32[]{:S(2)}) copy-start(f32[16,256]{1,0:T(8,128)} %copy-done.10) | copy-start | bytes 49156
  554.8 31.6 %copy-start.13 = (f32[16,256]{1,0:T(8,128)S(1)}, f32[16,256]{1,0:T(8,128)}, u32[]{:S(2)}) copy-start(f32[16,256]{1,0:T(8,128)} %copy-done.12) | copy-start | bytes 49156
  554.8 31.6 %copy-start.29 = (f32[16]{0:T(128)S(1)}, f32[16]{0:T(128)}, u32[]{:S(2)}) copy-start(f32[16]{0:T(128)} %copy-done.28) | copy-start | bytes 196
  554.8 31.6 %copy-start.31 = (f32[16]{0:T(128)S(1)}, f32[16]{0:T(128)}, u32[]{:S(2)}) copy-start(f32[16]{0:T(128)} %copy-done.30) | copy-start | bytes 196
  554.9 31.6 %copy-start.33 = (f32[16]{0:T(128)S(1)}, f32[16]{0:T(128)}, u32[]{:S(2)}) copy-start(f32[16]{0:T(128)} %copy-done.32) | copy-start | bytes 196
  554.9 31.6 %copy-start.35 = (f32[16,256]{1,0:T(8,128)S(1)}, f32[16,256]{1,0:T(8,128)}, u32[]{:S(2)}) copy-start(f32[16,256]{1,0:T(8,128)} %param.13) | copy-start | bytes 49156
  559.9 26.5 %collective-permute-start.5 = (f32[16,128,256]{2,1,0:T(8,128)S(1)}, f32[16,128,256]{2,1,0:T(8,128)S(1)}, u32[]{:S(2)}, u32[]{:S(2)}) collective-permute-start(f32[16,128,256]{2,1,0:T(8,128)S(1)} %slice.133), channel_id=1, source_target_pairs={{0,1},{1,2},{2,3},{3,4},{4,5},{5,6},{6,7},{7,8},{8,9},{9,10},{10,1... | collective-permute-start | bytes 6291464 | tf_op jit(solution)/shard_map/ppermute | solution.py:15
  586.5 73.9 %copy-start.37 = (f32[128]{0:T(128)S(1)}, f32[128]{0:T(128)}, u32[]{:S(2)}) copy-start(f32[128]{0:T(128)} %copy-done.36) | copy-start | bytes 1540
  586.5 73.9 %copy-start.1 = (f32[16,128,256]{2,1,0:T(8,128)S(1)}, f32[16,128,256]{2,1,0:T(8,128)}, u32[]{:S(2)}) copy-start(f32[16,128,256]{2,1,0:T(8,128)} %param.10) | copy-start | bytes 6291460
  586.5 73.9 %copy-start.18 = (f32[16]{0:T(128)S(1)}, f32[16]{0:T(128)}, u32[]{:S(2)}) copy-start(f32[16]{0:T(128)} %copy-done.16) | copy-start | bytes 196
  586.5 73.9 %copy-start.27 = (f32[128]{0:T(128)S(1)}, f32[128]{0:T(128)}, u32[]{:S(2)}) copy-start(f32[128]{0:T(128)} %copy-done.26) | copy-start | bytes 1540
where the time goes:
time: 673 us; the launch traced here: 667 us
  matrix products  438 us (65%)
  blocking collectives  128 us (19%)
  starting transfers between devices  47.3 us (7%)
  other arithmetic  29.9 us (4%)
  waiting for transfers between devices  11.9 us (2%)
  local copies, waits for them, and re-layouts  7.56 us (1%)
    dot_general x2, matrix products, apply_forward(): jnp.einsum('tpq,tmq->tmp', tiles, values, precision=highest_precision)  168 us
    dot_general x2, matrix products, apply_backward(): jnp.einsum('tpq,tmp->tmq', tiles, values, precision=highest_precision)  160 us
    psum x2, blocking collectives, squares(): return lax.psum(jnp.sum(vector * vector, axis=(0, 2)), 'reg')  79.8 us
    dot_general x2, matrix products, local(): jnp.einsum('bpq,bmq->bmp', diag_tiles, scaled, precision=highest_precision)  50.5 us
    psum x1, blocking collectives, local(): curvature = lax.psum(jnp.sum(direction * applied, axis=(0, 2)), 'reg')  48.7 us
    ppermute x6, starting transfers between devices, passed_along(): return lax.ppermute(shard, axis, pairs)  47.3 us
    dot_general x4, matrix products, place_rows(): return jnp.einsum('ts,tmp->smp', select, terms, precision=highest_precision)  31.5 us
    dot_general x4, matrix products, pick_rows(): jnp.einsum('ts,smq->tmq', select, values, precision=highest_precision)  28.2 us
  transfers between devices with their start and end apart: 6, of which 3 were waited for; matrix products, arithmetic and copies ran while one was open for 2% of the time, Pallas kernels for 0%

commit v1 on v0

v1 whole, which is shorter than its diff:
```python
import functools

import jax
import jax.numpy as jnp
from jax import lax
from jax.experimental import pallas as pl
from jax.experimental.pallas import tpu as pltpu
from jax.sharding import PartitionSpec as P

SIDE_MAX = 46
SLOTS = 4
ROWS = 32
MESH = pl.DeviceIdType.MESH
VMEM_BYTES = 56 * 1024 * 1024
VMEM = pl.BlockSpec(memory_space=pltpu.VMEM)
SMEM = pl.BlockSpec(memory_space=pltpu.SMEM)
ANY = pl.BlockSpec(memory_space=pl.ANY)


def passed_along(shard, axis, by):
    length = lax.axis_size(axis)
    pairs = [(i, i + by) for i in range(length) if 0 <= i + by < length]
    return lax.ppermute(shard, axis, pairs)


def split_rows(values):
    high = values.astype(jnp.bfloat16)
    low = (values - high.astype(jnp.float32)).astype(jnp.bfloat16)
    return high, low


def product(stacked, tile_high, tile_low, contract):
    members = stacked.shape[0] // 2
    dims = (((1,), (contract,)), ((), ()))
    first = lax.dot_general(stacked, tile_high, dims, preferred_element_type=jnp.float32)
    second = lax.dot_general(
        stacked[:members], tile_low, dims, preferred_element_type=jnp.float32
    )
    return first[:members] + first[members:] + second


def build_tile(pos_src, src, pos_dst, dst, cls_src, cls_dst, amp_ref, scale_ref, tile_ref):
    size = pos_dst.shape[2]
    columns = [
        jnp.transpose(jnp.broadcast_to(pos_src[axis, pl.ds(src, 1), :], (8, size)))
        for axis in range(2)
    ]
    rows = [pos_dst[axis, pl.ds(dst, 1), :] for axis in range(2)]
    classes = []
    for k in range(amp_ref.shape[1]):
        weight = amp_ref[cls_src, k] * amp_ref[cls_dst, k]
        scale = scale_ref[0, k]
        inv = scale_ref[1, k]
        inv2 = inv * inv
        classes.append(
            (
                scale,
                2.0 * scale,
                -0.5 * scale * scale,
                weight * inv2 * inv2 * inv * (1.0 / 12.0),
                weight,
                weight * inv2 * (-5.0 / 3.0),
                weight * inv2 * inv * 0.625,
                weight * inv2 * inv2 * 0.5,
                weight * inv2 * inv2 * inv * -0.25,
            )
        )
    for start in range(0, size, ROWS):
        part = slice(start, start + ROWS)
        east = columns[0][part, :1] - rows[0]
        north = columns[1][part, :1] - rows[1]
        square = east * east + north * north
        inverse = lax.rsqrt(jnp.maximum(square, 1e-30))
        dist = square * inverse
        total = None
        for scale, twice, shift, out_w, c0, c2, c3, c4, c5 in classes:
            inner = c0 + square * (c2 + dist * (c3 + dist * (c4 + dist * c5)))
            gap = jnp.maximum(twice - dist, 0.0)
            gap = gap * gap
            outer = (gap * gap) * ((square + dist * twice + shift) * (inverse * out_w))
            term = jnp.where(dist <= scale, inner, outer)
            total = term if total is None else total + term
        high, low = split_rows(total)
        tile_ref[0, part, :] = high
        tile_ref[1, part, :] = low


def tile_loop(build, base, count, tiles_ref, slots, sems, make, use):
    def copy(t):
        slot = lax.rem(t, SLOTS)
        if build:
            return pltpu.make_async_copy(slots.at[slot], tiles_ref.at[base + t], sems.at[slot])
        return pltpu.make_async_copy(tiles_ref.at[base + t], slots.at[slot], sems.at[slot])

    if build:

        def step(t, carry):
            slot = lax.rem(t, SLOTS)

            @pl.when(t >= SLOTS)
            def _():
                copy(t - SLOTS).wait()

            make(t, slots.at[slot])
            copy(t).start()
            use(t, slots.at[slot])
            return carry

        lax.fori_loop(0, count, step, 0)

        def drain(t, carry):
            copy(t).wait()
            return carry

        lax.fori_loop(jnp.maximum(count - SLOTS, 0), count, drain, 0)
    else:

        def warm(t, carry):
            copy(t).start()
            return carry

        lax.fori_loop(0, jnp.minimum(count, SLOTS - 1), warm, 0)

        def step(t, carry):
            @pl.when(t + SLOTS - 1 < count)
            def _():
                copy(t + SLOTS - 1).start()

            copy(t).wait()
            use(t, slots.at[lax.rem(t, SLOTS)])
            return carry

        lax.fori_loop(0, count, step, 0)


def stage_values(values, stacked):
    for start, blocks, block_of in values:

        def step(b, carry):
            members = stacked.shape[1] // 2
            high, low = split_rows(block_of(b))
            stacked[start + b, :members, :] = high
            stacked[start + b, members:, :] = low
            return carry

        lax.fori_loop(0, blocks, step, 0)


def mixed(coef_ref, base_ref, image_ref):
    if coef_ref is None:
        return lambda b: base_ref[b]

    def block(b):
        keep = jnp.concatenate([coef_ref[0], coef_ref[0]], axis=1)
        take = jnp.concatenate([coef_ref[1], coef_ref[1]], axis=1)
        return keep * base_ref[b] - take * image_ref[b]

    return block


def own_kernel(build, entries, *refs):
    if build:
        info, amp, scale, pos, base, tiles, acc, stacked, slots, sems = refs
        coef = image = None
    else:
        info, coef, base, image, tiles, acc, stacked, slots, sems = refs
    local_pairs = info[2 * entries]
    live = info[2 * entries + 2]
    blocks = base.shape[0]
    acc[...] = jnp.zeros_like(acc)
    stage_values([(0, blocks, mixed(coef, base, image))], stacked)

    def ends(t):
        entry = jnp.clip(t - live, 0, entries - 1)
        src = jnp.where(t < live, t, info[entry])
        dst = jnp.where(t < live, t, info[entries + entry])
        return src, dst

    def make(t, tile):
        src, dst = ends(t)
        first = 2 * entries + 3
        build_tile(pos, src, pos, dst, info[first + src], info[first + dst], amp, scale, tile)

    def use(t, tile):
        src, dst = ends(t)
        acc[dst] += product(stacked[src], tile[0], tile[1], 0)

        @pl.when(t >= live)
        def _():
            acc[src] += product(stacked[dst], tile[0], tile[1], 1)

    tile_loop(build, 0, live + local_pairs, tiles, slots, sems, make, use)


def cross_kernel(build, entries, *refs):
    if build:
        (info, info_n, info_s, amp, scale, pos, pos_two, base_n, base_s, acc_in, sigma, obs_var,
         direct, tiles_in, tiles, image_out, scaled_out, sums, stacked, slots, sems, parts) = refs
        coef = image_n = image_s = image = None
    else:
        (info, info_n, info_s, coef, base_n, image_n, base_s, image_s, acc_in, sigma, obs_var,
         direct, image, tiles, image_out, sums, stacked, slots, sems, parts) = refs
    blocks = acc_in.shape[0]
    local_pairs = info[2 * entries]
    north_pairs = info[2 * entries + 1]
    local_south = info_s[2 * entries]
    south_pairs = info_s[2 * entries + 1]
    image_out[...] = acc_in[...]
    stage_values(
        [
            (0, blocks, mixed(coef, base_n, image_n)),
            (blocks, blocks, mixed(coef, base_s, image_s)),
        ],
        stacked,
    )

    def ends(t):
        is_north = t < north_pairs
        entry_n = jnp.clip(local_pairs + t, 0, entries - 1)
        entry_s = jnp.clip(local_south + t - north_pairs, 0, entries - 1)
        far_n = info[entries + entry_n]
        far_s = info_s[entry_s]
        dst = jnp.where(is_north, info[entry_n], info_s[entries + entry_s])
        return is_north, far_n, far_s, dst

    def make(t, tile):
        is_north, far_n, far_s, dst = ends(t)
        first = 2 * entries + 3
        src = jnp.where(is_north, far_n, blocks + far_s)
        cls_src = jnp.where(is_north, info_n[first + far_n], info_s[first + far_s])
        build_tile(pos_two, src, pos, dst, cls_src, info[first + dst], amp, scale, tile)

    def use(t, tile):
        is_north, far_n, far_s, dst = ends(t)
        src = jnp.where(is_north, far_n, blocks + far_s)
        image_out[dst] += product(stacked[src], tile[0], tile[1], 0)

    before = info[2 * entries + 2] + local_pairs
    tile_loop(build, before, north_pairs + south_pairs, tiles, slots, sems, make, use)

    parts[...] = jnp.zeros_like(parts)
    direction_of = mixed(coef, direct, image)
    half = parts.shape[2]

    def finish(b, carry):
        weight = sigma[pl.ds(b, 1), :]
        direction = direction_of(b)
        result = weight * image_out[b] + obs_var[pl.ds(b, 1), :] * direction
        image_out[b] = result
        if build:
            scaled_out[b] = weight * result
        terms = [direction * result]
        if build:
            terms += [direction * direction, result * result]
        for k, term in enumerate(terms):
            parts[k] += term[:, :half] + term[:, half:]
        return carry

    lax.fori_loop(0, blocks, finish, 0)
    sums[...] = jnp.zeros_like(sums)
    for k in range(3 if build else 1):
        sums[k : k + 1, :] = jnp.sum(jnp.transpose(parts[k]), axis=0, keepdims=True)


def total_kernel(n, value, out, held, send_sems, recv_sems):
    me = lax.axis_index("reg")
    stages = n.bit_length() - 1
    barrier = pltpu.get_barrier_semaphore()

    def partner(stage):
        step = 1 << stage
        upper = lax.rem(lax.div(me, step), 2)
        return me + step - 2 * step * upper

    for stage in range(stages):
        pl.semaphore_signal(
            barrier, inc=1, device_id={"reg": partner(stage)}, device_id_type=MESH
        )
    pl.semaphore_wait(barrier, stages)
    held[0] = value[...]
    for stage in range(stages):
        copy = pltpu.make_async_remote_copy(
            src_ref=held.at[2 * stage],
            dst_ref=held.at[2 * stage + 1],
            send_sem=send_sems.at[stage],
            recv_sem=recv_sems.at[stage],
            device_id={"reg": partner(stage)},
            device_id_type=MESH,
        )
        copy.start()
        copy.wait()
        held[2 * stage + 2] = held[2 * stage] + held[2 * stage + 1]
    out[...] = held[2 * stages]


def total_over(value, call):
    n = lax.axis_size("reg")
    if n & (n - 1):
        return lax.psum(value, "reg")
    stages = n.bit_length() - 1
    return pl.pallas_call(
        functools.partial(total_kernel, n),
        out_shape=jax.ShapeDtypeStruct(value.shape, value.dtype),
        in_specs=[VMEM],
        out_specs=VMEM,
        scratch_shapes=[
            pltpu.VMEM((2 * stages + 1,) + value.shape, value.dtype),
            pltpu.SemaphoreType.DMA((stages,)),
            pltpu.SemaphoreType.DMA((stages,)),
        ],
        compiler_params=pltpu.CompilerParams(collective_id=call, has_side_effects=True),
        name="member_sums_%d" % call,
    )(value)


def local(
    obs_value,
    positions,
    sigma,
    obs_var,
    class_amp,
    length_scale,
    block_class,
    block_count,
    pair_list,
    pair_count,
):
    blocks, members, size = obs_value.shape
    entries = pair_list.shape[1]
    info = jnp.concatenate(
        [pair_list[0], pair_list[1], pair_count[:, 0], block_count, block_class]
    )
    width = info.shape[0]
    packed = jnp.concatenate(
        [
            positions.reshape(2 * blocks, size),
            jnp.pad(info.astype(jnp.float32), (0, -width % size)).reshape(-1, size),
        ]
    )
    packed_n = passed_along(packed, "reg", -1)
    packed_s = passed_along(packed, "reg", 1)
    pos_n, pos_s = (p[: 2 * blocks].reshape(2, blocks, size) for p in (packed_n, packed_s))
    info_n, info_s = (
        p[2 * blocks :].reshape(-1)[:width].astype(jnp.int32) for p in (packed_n, packed_s)
    )
    pos_two = jnp.concatenate([pos_n, pos_s], axis=1)
    scales = jnp.stack([length_scale, 1.0 / length_scale])

    live = (jnp.arange(blocks, dtype=jnp.int32) < block_count[0]).astype(jnp.float32)
    first_residual = obs_value * live[:, None, None]
    scaled = sigma[:, None, :] * first_residual
    scaled_n = passed_along(scaled, "reg", -1)
    scaled_s = passed_along(scaled, "reg", 1)

    own_cap = blocks + min(SIDE_MAX, entries)
    cross_cap = 2 * min(SIDE_MAX, entries)
    cap = blocks + entries + min(SIDE_MAX, entries)
    array = jax.ShapeDtypeStruct((blocks, members, size), jnp.float32)
    sums_shape = jax.ShapeDtypeStruct((8, members), jnp.float32)

    tiles_shape = jax.ShapeDtypeStruct((cap, 2, size, size), jnp.bfloat16)

    def scratch(count):
        return [
            pltpu.VMEM((count, 2 * members, size), jnp.bfloat16),
            pltpu.VMEM((SLOTS, 2, size, size), jnp.bfloat16),
            pltpu.SemaphoreType.DMA((SLOTS,)),
        ]

    parts = [pltpu.VMEM((3, members, size // 2), jnp.float32)]
    params = pltpu.CompilerParams(vmem_limit_bytes=VMEM_BYTES)

    def cost(count, build):
        return pl.CostEstimate(
            flops=count * 6 * size * size * members + build * count * 80 * size * size,
            bytes_accessed=count * 4 * size * size,
            transcendentals=build * count * size * size,
        )

    tiles, spread = pl.pallas_call(
        functools.partial(own_kernel, True, entries),
        out_shape=[tiles_shape, array],
        in_specs=[SMEM, SMEM, SMEM, VMEM, VMEM],
        out_specs=[ANY, VMEM],
        scratch_shapes=scratch(blocks),
        compiler_params=params,
        cost_estimate=cost(own_cap, 1),
        name="own_tiles_and_spread",
    )(info, class_amp, scales, positions, scaled)
    tiles, image, scaled_image, sums = pl.pallas_call(
        functools.partial(cross_kernel, True, entries),
        out_shape=[tiles_shape, array, array, sums_shape],
        in_specs=[SMEM] * 5 + [VMEM] * 8 + [ANY],
        out_specs=[ANY, VMEM, VMEM, VMEM],
        input_output_aliases={13: 0},
        scratch_shapes=scratch(2 * blocks) + parts,
        compiler_params=params,
        cost_estimate=cost(cross_cap, 1),
        name="cross_tiles_and_image",
    )(
        info, info_n, info_s, class_amp, scales, positions, pos_two, scaled_n, scaled_s, spread,
        sigma, obs_var, first_residual, tiles,
    )
    image_n = passed_along(scaled_image, "reg", -1)
    image_s = passed_along(scaled_image, "reg", 1)
    totals = total_over(sums, 0)
    curvature, norm = totals[0], totals[1]
    step = norm / curvature
    norm_next = jnp.maximum(norm - 2.0 * step * curvature + step * step * totals[2], 0.0)
    keep = 1.0 + norm_next / norm
    coef = jnp.broadcast_to(jnp.stack([keep, step])[:, :, None], (2, members, size // 2))

    spread = pl.pallas_call(
        functools.partial(own_kernel, False, entries),
        out_shape=array,
        in_specs=[SMEM, VMEM, VMEM, VMEM, ANY],
        out_specs=VMEM,
        scratch_shapes=scratch(blocks),
        compiler_params=params,
        cost_estimate=cost(own_cap, 0),
        name="own_spread",
    )(info, coef, scaled, scaled_image, tiles)
    image_two, sums = pl.pallas_call(
        functools.partial(cross_kernel, False, entries),
        out_shape=[array, sums_shape],
        in_specs=[SMEM] * 3 + [VMEM] * 10 + [ANY],
        out_specs=[VMEM, VMEM],
        scratch_shapes=scratch(2 * blocks) + parts,
        compiler_params=params,
        cost_estimate=cost(cross_cap, 0),
        name="cross_image",
    )(
        info, info_n, info_s, coef, scaled_n, image_n, scaled_s, image_s, spread, sigma, obs_var,
        first_residual, image, tiles,
    )
    step_two = norm_next / total_over(sums, 1)[0]
    along = lambda member_values: member_values[None, :, None]
    direction_two = along(keep) * first_residual - along(step) * image
    weights = along(step) * first_residual + along(step_two) * direction_two
    residual = first_residual - along(step) * image - along(step_two) * image_two
    return (weights, residual)


def solution(mesh):
    placed = (
        P(("grp", "reg"), None, None),
        P(None, ("grp", "reg"), None),
        P(("grp", "reg"), None),
        P(("grp", "reg"), None),
        P(),
        P(),
        P(("grp", "reg")),
        P(("grp", "reg")),
        P(None, ("grp", "reg")),
        P(None, ("grp", "reg")),
    )
    return jax.shard_map(
        local,
        mesh=mesh,
        in_specs=placed,
        out_specs=(P(("grp", "reg"), None, None), P(("grp", "reg"), None, None)),
        check_vma=False,
    )
```

time: 673 us -> 255 us (0.38)
  the two profiles are of different devices: /device:TPU:0 before, /device:TPU:6 now
where the time goes in v1:
time: 255 us; the launch traced here: 253 us
  Pallas kernels  209 us (82%)
  starting transfers between devices  16.7 us (7%)
  other arithmetic  12.7 us (5%)
  waiting for transfers between devices  10.3 us (4%)
    pallas_call x2, Pallas kernels, total_over(): pl.pallas_call(functools.partial(total_kernel, n), out_shape=jax.ShapeDty...  104 us
    pallas_call x1, Pallas kernels, local(): pl.pallas_call(functools.partial(cross_kernel, True, entries), out_shape=...  43.9 us
    pallas_call x1, Pallas kernels, local(): pl.pallas_call(functools.partial(own_kernel, True, entries), out_shape=[t...  28.5 us
    pallas_call x1, Pallas kernels, local(): pl.pallas_call(functools.partial(cross_kernel, False, entries), out_shape...  20.1 us
    ppermute x6, starting transfers between devices, passed_along(): return lax.ppermute(shard, axis, pairs)  16.7 us
    pallas_call x1, Pallas kernels, local(): pl.pallas_call(functools.partial(own_kernel, False, entries), out_shape=a...  13.3 us
    ppermute x6, waiting for transfers between devices, passed_along(): return lax.ppermute(shard, axis, pairs)  10.3 us
    sub x1, other arithmetic, local(): first_residual - along(step) * image - along(step_two) * image_two  5.29 us
  transfers between devices with their start and end apart: 6, of which 1 were waited for; matrix products, arithmetic and copies ran while one was open for 2% of the time, Pallas kernels for 41%

profile of v1, /device:TPU:6, one launch (start us, length us, event | category | flops | bytes accessed | tf_op | source)
XLA Modules:
  0.0 252.8 jit_solution(15944715053658869599)
XLA Ops:
  1.3 0.0 copy-start.6
  1.3 0.0 copy-start.7
  1.3 0.0 copy-start.8
  1.3 0.0 copy-start.3
  1.3 0.0 copy-start.9
  1.3 3.5 %broadcast_multiply_fusion.1 = (f32[16,128,256]{2,1,0:T(8,128)S(1)}, f32[16,128,256]{2,1,0:T(8,128)}) fusion(f32[16,256]{1,0:T(8,128)} %refs_9_.1, f32[16,128,256]{2,1,0:T(8,128)} %param.10, f32[16]{0:T(128)S(1)} %compare_convert_fusion), kind=kLoop, calls=%fused_computation.3 | loop fusion | flops 1048576 | bytes 6307904 | tf_op jit(solution)/shard_map/mul | solution.py:351
  4.8 0.0 copy-start.1
  4.8 1.9 collective-permute-start.3
  6.8 3.6 %collective-permute-start.2 = (f32[16,128,256]{2,1,0:T(8,128)S(1)}, f32[16,128,256]{2,1,0:T(8,128)}, u32[]{:S(2)}, u32[]{:S(2)}) collective-permute-start(f32[16,128,256]{2,1,0:T(8,128)S(1)} %get-tuple-element.23.refs_4_.refs_2_), channel_id=1, source_target_pairs={{1,0},{2,1},{3,2},{4,3},{5,4},{6,5},{7,6},{8,7},{9,8},{10,9},{11,1... | collective-permute-start | bytes 6291464 | tf_op jit(solution)/shard_map/ppermute | solution.py:23
  10.4 0.0 copy-done.6
  10.4 0.0 copy-done.7
  10.4 0.0 copy-done.8
  10.4 0.1 concatenate.9.refs_0_
  10.5 0.0 copy-start.4
  10.5 0.0 copy-done.3
  10.6 1.9 collective-permute-start.1
  12.5 3.6 %collective-permute-start = (f32[33,256]{1,0:T(8,128)S(1)}, f32[33,256]{1,0:T(8,128)S(1)}, u32[]{:S(2)}, u32[]{:S(2)}) collective-permute-start(f32[33,256]{1,0:T(8,128)S(1)} %pad_maximum_fusion.1), channel_id=1, source_target_pairs={{1,0},{2,1},{3,2},{4,3},{5,4},{6,5},{7,6},{8,7},{9,8},{10,9},{11,1... | collective-permute-start | bytes 101384 | tf_op jit(solution)/shard_map/ppermute | solution.py:23
  16.1 0.0 copy-done.9
  16.2 0.6 pad_maximum_fusion.2.refs_2_.refs_4_
  16.8 0.0 copy-done.1
  16.8 0.0 copy-done.4
  16.8 28.5 %own_tiles_and_spread.1 = (bf16[123,2,256,256]{3,2,1,0:T(8,128)(2,1)}, f32[16,128,256]{2,1,0:T(8,128)}) custom-call(s32[141]{0:T(256)} %copy-done.4, f32[3,3]{1,0:T(4,128)} %refs_3_.3, f32[2,3]{1,0:T(2,128)} %pad_maximum_fusion.2.refs_2_.refs_4_, f32[2,16,256]{2,1,0:T(8,128)} %refs_5_.1, f32[16,128,256]{2,1,0:T(8,128)} %copy-done.1), custom_call_target="tpu_custom_call" | custom-call | flops 3445620736 | bytes 16252928 | tf_op jit(solution)/shard_map/own_tiles_and_spread/pallas_call | solution.py:380
  45.3 10.3 %collective-permute-done.1 = f32[33,256]{1,0:T(8,128)S(1)} collective-permute-done((f32[33,256]{1,0:T(8,128)S(1)}, f32[33,256]{1,0:T(8,128)S(1)}, u32[]{:S(2)}, u32[]{:S(2)}) %collective-permute-start.1) | collective-permute-done | bytes 33824 | tf_op jit(solution)/shard_map/ppermute | solution.py:23
  55.5 0.0 collective-permute-done
  55.5 0.6 pad_maximum_fusion.refs_6_
  56.2 0.6 slice_convert_fusion
  56.8 0.6 slice_convert_fusion.1
  57.4 0.0 collective-permute-done.3.refs_8_.refs_6_
  57.4 0.0 collective-permute-done.2.refs_7_.refs_4_
  57.4 43.9 %cross_tiles_and_image.1 = (bf16[123,2,256,256]{3,2,1,0:T(8,128)(2,1)}, f32[16,128,256]{2,1,0:T(8,128)}, f32[16,128,256]{2,1,0:T(8,128)}, f32[8,128]{1,0:T(8,128)}) custom-call(s32[141]{0:T(256)} %copy-done.4, s32[141]{0:T(256)} %bitcast.47, s32[141]{0:T(256)} %bitcast.45, f32[3,3]{1,0:T(4,128)} %refs_3_.3, ...), custom_call_target="tpu_custom_call", output_to_operand_aliasing={{0}: (13, {})} | custom-call | flops 5112856576 | bytes 24117248 | tf_op jit(solution)/shard_map/cross_tiles_and_image/pallas_call | solution.py:390
  101.3 1.9 collective-permute-start.5
  103.2 3.6 %collective-permute-start.4 = (f32[16,128,256]{2,1,0:T(8,128)}, f32[16,128,256]{2,1,0:T(8,128)}, u32[]{:S(2)}, u32[]{:S(2)}) collective-permute-start(f32[16,128,256]{2,1,0:T(8,128)} %get-tuple-element.13.refs_3_), channel_id=1, source_target_pairs={{1,0},{2,1},{3,2},{4,3},{5,4},{6,5},{7,6},{8,7},{9,8},{10,9},{11,1... | collective-permute-start | bytes 6291464 | tf_op jit(solution)/shard_map/ppermute | solution.py:23
  106.9 61.2 %member_sums_0.1 = f32[8,128]{1,0:T(8,128)} custom-call(f32[8,128]{1,0:T(8,128)} %get-tuple-element.12.value), custom_call_target="tpu_custom_call" | custom-call | tf_op jit(solution)/shard_map/member_sums_0/pallas_call | solution.py:301
  168.1 0.8 fusion.4
  168.9 0.7 broadcast_in_dim.2.refs_1_.refs_3_
  169.6 13.3 %own_spread.1.refs_8_ = f32[16,128,256]{2,1,0:T(8,128)} custom-call(s32[141]{0:T(256)} %copy-done.4, f32[2,128,128]{2,1,0:T(8,128)} %broadcast_in_dim.2.refs_1_.refs_3_, f32[16,128,256]{2,1,0:T(8,128)} %copy-done.1, f32[16,128,256]{2,1,0:T(8,128)} %get-tuple-element.13.refs_3_, bf16[123,2,256,256]{3,2,1,0:T(8,128)(2,1)} %get-tuple-element.14.refs_4_.refs_13_), custom_call_target="tpu_custom_call" | custom-call | flops 3120562176 | bytes 16252928 | tf_op jit(solution)/shard_map/own_spread/pallas_call | solution.py:413
  182.9 0.0 collective-permute-done.5.refs_7_
  182.9 0.0 copy-start.2
  182.9 0.0 collective-permute-done.4.refs_5_
  183.0 1.3 copy-done.2
  184.3 0.0 copy-start.5
  184.3 0.0 copy-start
  184.3 20.1 %cross_image.1 = (f32[16,128,256]{2,1,0:T(8,128)}, f32[8,128]{1,0:T(8,128)}) custom-call(s32[141]{0:T(256)} %copy-done.4, s32[141]{0:T(256)} %bitcast.48, s32[141]{0:T(256)} %bitcast.46, f32[2,128,128]{2,1,0:T(8,128)} %broadcast_in_dim.2.refs_1_.refs_3_, f32[16,128,256]{2,1,0:T(8,128)} %collective-permute-done.2.refs_7_.refs_4_, ...), custom_call_target="tpu_custom_call" | custom-call | flops 4630511616 | bytes 24117248 | tf_op jit(solution)/shard_map/cross_image/pallas_call | solution.py:423
  204.4 42.4 %member_sums_1.1 = f32[8,128]{1,0:T(8,128)} custom-call(f32[8,128]{1,0:T(8,128)} %get-tuple-element.16.value), custom_call_target="tpu_custom_call" | custom-call | tf_op jit(solution)/shard_map/member_sums_1/pallas_call | solution.py:301
  246.8 0.0 copy-done.5
  246.8 0.7 bitcast_divide_fusion
  247.5 0.0 copy-done
  247.5 5.3 %multiply_subtract_fusion = (f32[16,128,256]{2,1,0:T(8,128)}, f32[16,128,256]{2,1,0:T(8,128)}) fusion(f32[16,128,256]{2,1,0:T(8,128)} %get-tuple-element.17, f32[16,128,256]{2,1,0:T(8,128)S(1)} %copy-done, f32[16,128,256]{2,1,0:T(8,128)} %get-tuple-element.15.refs_12_, f32[128]{0:T(128)S(1)} %get-tuple-element.18, f32[128]{0:T(128)S(1)} %get-tuple-element.20, ...), kind=kLoop, calls=%fused_computation | loop fusion | flops 4718592 | bytes 10487296 | tf_op jit(solution)/shard_map/sub | solution.py:440
  (10 shorter events, 0.1 us)
Async XLA Ops:
  1.3 9.1 %copy-start.6 = (s32[2,61]{1,0:T(2,128)S(1)}, s32[2,61]{1,0:T(2,128)}, u32[]{:S(2)}) copy-start(s32[2,61]{1,0:T(2,128)} %param.18) | copy-start | bytes 1468
  1.3 9.1 %copy-start.7 = (s32[2,1]{0,1:T(1,128)S(1)}, s32[2,1]{0,1:T(1,128)}, u32[]{:S(2)}) copy-start(s32[2,1]{0,1:T(1,128)} %param.19) | copy-start | bytes 28
  1.3 9.1 %copy-start.8 = (s32[16]{0:T(128)S(1)}, s32[16]{0:T(128)}, u32[]{:S(2)}) copy-start(s32[16]{0:T(128)} %param.16) | copy-start | bytes 196
  1.3 9.2 %copy-start.3 = (f32[2,16,256]{2,1,0:T(8,128)S(1)}, f32[2,16,256]{2,1,0:T(8,128)}, u32[]{:S(2)}) copy-start(f32[2,16,256]{2,1,0:T(8,128)} %refs_5_.1) | copy-start | bytes 98308
  1.3 14.8 %copy-start.9 = (f32[3]{0:T(128)S(1)}, f32[3]{0:T(128)}, u32[]{:S(2)}) copy-start(f32[3]{0:T(128)} %param.15) | copy-start | bytes 40
  4.8 11.9 %copy-start.1 = (f32[16,128,256]{2,1,0:T(8,128)}, f32[16,128,256]{2,1,0:T(8,128)S(1)}, u32[]{:S(2)}) copy-start(f32[16,128,256]{2,1,0:T(8,128)S(1)} %get-tuple-element.23.refs_4_.refs_2_) | copy-start | bytes 6291460
  4.8 52.5 %collective-permute-start.3 = (f32[16,128,256]{2,1,0:T(8,128)S(1)}, f32[16,128,256]{2,1,0:T(8,128)}, u32[]{:S(2)}, u32[]{:S(2)}) collective-permute-start(f32[16,128,256]{2,1,0:T(8,128)S(1)} %get-tuple-element.23.refs_4_.refs_2_), channel_id=1, source_target_pairs={{0,1},{1,2},{2,3},{3,4},{4,5},{5,6},{6,7},{7,8},{8,9},{9,10},{10,1... | collective-permute-start | bytes 6291464 | tf_op jit(solution)/shard_map/ppermute | solution.py:23
  6.8 50.6 %collective-permute-start.2 = (f32[16,128,256]{2,1,0:T(8,128)S(1)}, f32[16,128,256]{2,1,0:T(8,128)}, u32[]{:S(2)}, u32[]{:S(2)}) collective-permute-start(f32[16,128,256]{2,1,0:T(8,128)S(1)} %get-tuple-element.23.refs_4_.refs_2_), channel_id=1, source_target_pairs={{1,0},{2,1},{3,2},{4,3},{5,4},{6,5},{7,6},{8,7},{9,8},{10,9},{11,1... | collective-permute-start | bytes 6291464 | tf_op jit(solution)/shard_map/ppermute | solution.py:23
  10.5 6.2 %copy-start.4 = (s32[141]{0:T(256)}, s32[141]{0:T(256)S(1)}, u32[]{:S(2)}) copy-start(s32[141]{0:T(256)S(1)} %concatenate.9.refs_0_) | copy-start | bytes 1696
  10.6 45.0 %collective-permute-start.1 = (f32[33,256]{1,0:T(8,128)S(1)}, f32[33,256]{1,0:T(8,128)S(1)}, u32[]{:S(2)}, u32[]{:S(2)}) collective-permute-start(f32[33,256]{1,0:T(8,128)S(1)} %pad_maximum_fusion.1), channel_id=1, source_target_pairs={{0,1},{1,2},{2,3},{3,4},{4,5},{5,6},{6,7},{7,8},{8,9},{9,10},{10,1... | collective-permute-start | bytes 101384 | tf_op jit(solution)/shard_map/ppermute | solution.py:23
  12.5 43.0 %collective-permute-start = (f32[33,256]{1,0:T(8,128)S(1)}, f32[33,256]{1,0:T(8,128)S(1)}, u32[]{:S(2)}, u32[]{:S(2)}) collective-permute-start(f32[33,256]{1,0:T(8,128)S(1)} %pad_maximum_fusion.1), channel_id=1, source_target_pairs={{1,0},{2,1},{3,2},{4,3},{5,4},{6,5},{7,6},{8,7},{9,8},{10,9},{11,1... | collective-permute-start | bytes 101384 | tf_op jit(solution)/shard_map/ppermute | solution.py:23
  101.3 81.6 %collective-permute-start.5 = (f32[16,128,256]{2,1,0:T(8,128)}, f32[16,128,256]{2,1,0:T(8,128)S(1)}, u32[]{:S(2)}, u32[]{:S(2)}) collective-permute-start(f32[16,128,256]{2,1,0:T(8,128)} %get-tuple-element.13.refs_3_), channel_id=1, source_target_pairs={{0,1},{1,2},{2,3},{3,4},{4,5},{5,6},{6,7},{7,8},{8,9},{9,10},{10,1... | collective-permute-start | bytes 6291464 | tf_op jit(solution)/shard_map/ppermute | solution.py:23
  103.2 79.7 %collective-permute-start.4 = (f32[16,128,256]{2,1,0:T(8,128)}, f32[16,128,256]{2,1,0:T(8,128)}, u32[]{:S(2)}, u32[]{:S(2)}) collective-permute-start(f32[16,128,256]{2,1,0:T(8,128)} %get-tuple-element.13.refs_3_), channel_id=1, source_target_pairs={{1,0},{2,1},{3,2},{4,3},{5,4},{6,5},{7,6},{8,7},{9,8},{10,9},{11,1... | collective-permute-start | bytes 6291464 | tf_op jit(solution)/shard_map/ppermute | solution.py:23
  182.9 1.3 copy-start.2
  184.3 62.5 %copy-start.5 = (f32[8,128]{1,0:T(8,128)S(1)}, f32[8,128]{1,0:T(8,128)}, u32[]{:S(2)}) copy-start(f32[8,128]{1,0:T(8,128)} %member_sums_0.1) | copy-start | bytes 12292
  184.3 63.2 %copy-start = (f32[16,128,256]{2,1,0:T(8,128)S(1)}, f32[16,128,256]{2,1,0:T(8,128)}, u32[]{:S(2)}) copy-start(f32[16,128,256]{2,1,0:T(8,128)} %get-tuple-element.24.refs_12_.refs_11_) | copy-start | bytes 6291460

commit v2 on v1

v2 whole, which is shorter than its diff:
```python
import functools

import jax
import jax.numpy as jnp
from jax import lax
from jax.experimental import pallas as pl
from jax.experimental.pallas import tpu as pltpu
from jax.sharding import PartitionSpec as P

SIDE_MAX = 46
SLOTS = 4
GROUP = 4
ROWS = 16
MESH = pl.DeviceIdType.MESH
VMEM_BYTES = 56 * 1024 * 1024
VMEM = pl.BlockSpec(memory_space=pltpu.VMEM)
SMEM = pl.BlockSpec(memory_space=pltpu.SMEM)
ANY = pl.BlockSpec(memory_space=pl.ANY)


def passed_along(shard, axis, by):
    length = lax.axis_size(axis)
    pairs = [(i, i + by) for i in range(length) if 0 <= i + by < length]
    return lax.ppermute(shard, axis, pairs)


def split_rows(values):
    high = values.astype(jnp.bfloat16)
    low = (values - high.astype(jnp.float32)).astype(jnp.bfloat16)
    return high, low


def product(stacked, tile_high, tile_low, contract):
    members = stacked.shape[0] // 2
    dims = (((1,), (contract,)), ((), ()))
    first = lax.dot_general(stacked, tile_high, dims, preferred_element_type=jnp.float32)
    second = lax.dot_general(
        stacked[:members], tile_low, dims, preferred_element_type=jnp.float32
    )
    return first[:members] + first[members:] + second


def build_tile(pos_src, src, pos_dst, dst, cls_src, cls_dst, amp_ref, scale_ref, tile_ref):
    size = pos_dst.shape[2]
    columns = [
        jnp.transpose(jnp.broadcast_to(pos_src[axis, pl.ds(src, 1), :], (8, size)))
        for axis in range(2)
    ]
    rows = [pos_dst[axis, pl.ds(dst, 1), :] for axis in range(2)]
    classes = []
    for k in range(amp_ref.shape[1]):
        weight = amp_ref[cls_src, k] * amp_ref[cls_dst, k]
        scale = scale_ref[0, k]
        inv = scale_ref[1, k]
        inv2 = inv * inv
        classes.append(
            (
                scale,
                2.0 * scale,
                -0.5 * scale * scale,
                weight * inv2 * inv2 * inv * (1.0 / 12.0),
                weight,
                weight * inv2 * (-5.0 / 3.0),
                weight * inv2 * inv * 0.625,
                weight * inv2 * inv2 * 0.5,
                weight * inv2 * inv2 * inv * -0.25,
            )
        )
    for start in range(0, size, ROWS):
        part = slice(start, start + ROWS)
        east = columns[0][part, :1] - rows[0]
        north = columns[1][part, :1] - rows[1]
        square = east * east + north * north
        inverse = lax.rsqrt(jnp.maximum(square, 1e-30))
        dist = square * inverse
        total = None
        for scale, twice, shift, out_w, c0, c2, c3, c4, c5 in classes:
            inner = c0 + square * (c2 + dist * (c3 + dist * (c4 + dist * c5)))
            gap = jnp.maximum(twice - dist, 0.0)
            gap = gap * gap
            outer = (gap * gap) * ((square + dist * twice + shift) * (inverse * out_w))
            term = jnp.where(dist <= scale, inner, outer)
            total = term if total is None else total + term
        high, low = split_rows(total)
        tile_ref[0, part, :] = high
        tile_ref[1, part, :] = low


def build_loop(base, count, tiles_ref, slots, sems, make, use):
    def slot_of(t):
        return slots.at[lax.rem(t, SLOTS)]

    def copy(t):
        return pltpu.make_async_copy(slot_of(t), tiles_ref.at[base + t], sems.at[lax.rem(t, SLOTS)])

    @pl.when(count > 0)
    def _():
        make(0, slots.at[0])
        copy(0).start()

    def step(t, carry):
        @pl.when(t >= SLOTS)
        def _():
            copy(t - SLOTS).wait()

        use([(t - 1, slot_of(t - 1))])
        make(t, slot_of(t))
        copy(t).start()
        return carry

    lax.fori_loop(1, count, step, 0)

    @pl.when(count > 0)
    def _():
        use([(count - 1, slot_of(count - 1))])

    def drain(t, carry):
        copy(t).wait()
        return carry

    lax.fori_loop(jnp.maximum(count - SLOTS, 0), count, drain, 0)


def read_loop(base, count, tiles_ref, slots, sems, use):
    groups = lax.div(count + GROUP - 1, GROUP)

    def copy(g):
        slot = lax.rem(g, 2)
        return pltpu.make_async_copy(
            tiles_ref.at[pl.ds(base + g * GROUP, GROUP)], slots.at[slot], sems.at[slot]
        )

    @pl.when(groups > 0)
    def _():
        copy(0).start()

    def step(g, carry):
        @pl.when(g + 1 < groups)
        def _():
            copy(g + 1).start()

        copy(g).wait()
        use([(g * GROUP + j, slots.at[lax.rem(g, 2), j]) for j in range(GROUP)])
        return carry

    lax.fori_loop(0, groups, step, 0)


def stage_values(start, count, base_ref, stacked):
    members = stacked.shape[1] // 2

    def step(b, carry):
        high, low = split_rows(base_ref[b])
        stacked[start + b, :members, :] = high
        stacked[start + b, members:, :] = low
        return carry

    lax.fori_loop(0, count, step, 0)


def add_all(acc, terms):
    for where, term in terms:
        acc[where] += term


def own_kernel(build, entries, *refs):
    if build:
        info, amp, scale, pos, base, tiles, acc, stacked, slots, sems = refs
    else:
        info, base, tiles, acc, stacked, slots, sems = refs
    live = info[2 * entries + 2]
    count = live + info[2 * entries]
    blocks = stacked.shape[0]
    acc[...] = jnp.zeros_like(acc)
    stage_values(0, blocks, base, stacked)

    def ends(t):
        entry = jnp.clip(t - live, 0, entries - 1)
        src = jnp.where(t < live, t, info[entry])
        dst = jnp.where(t < live, t, info[entries + entry])
        return src, dst

    def make(t, tile):
        src, dst = ends(t)
        first = 2 * entries + 3
        build_tile(pos, src, pos, dst, info[first + src], info[first + dst], amp, scale, tile)

    def use(items):
        terms = []
        for t, tile in items:
            src, dst = ends(t)
            to = jnp.where(t < count, dst, blocks)
            back = jnp.where(jnp.logical_and(t >= live, t < count), src, blocks)
            terms.append((to, product(stacked[src], tile[0], tile[1], 0)))
            terms.append((back, product(stacked[dst], tile[0], tile[1], 1)))
        add_all(acc, terms)

    if build:
        build_loop(0, count, tiles, slots, sems, make, use)
    else:
        read_loop(0, count, tiles, slots, sems, use)


def cross_kernel(build, entries, *refs):
    if build:
        (info, info_n, info_s, amp, scale, pos, pos_two, base_n, base_s, acc_in, sigma, obs_var,
         direct, tiles_in, tiles, image_out, scaled_out, sums, stacked, slots, sems, acc, parts) = refs
    else:
        (info, info_n, info_s, base_n, base_s, acc_in, sigma, obs_var,
         direct, sums_in, tiles, image_out, sums, stacked, slots, sems, acc, parts) = refs
    blocks = image_out.shape[0]
    local_pairs = info[2 * entries]
    north_pairs = info[2 * entries + 1]
    local_south = info_s[2 * entries]
    south_pairs = info_s[2 * entries + 1]
    count = north_pairs + south_pairs
    acc[...] = acc_in[...]
    stage_values(0, blocks, base_n, stacked)
    stage_values(blocks, blocks, base_s, stacked)

    def ends(t):
        is_north = t < north_pairs
        entry_n = jnp.clip(local_pairs + t, 0, entries - 1)
        entry_s = jnp.clip(local_south + t - north_pairs, 0, entries - 1)
        far_n = info[entries + entry_n]
        far_s = info_s[entry_s]
        dst = jnp.where(is_north, info[entry_n], info_s[entries + entry_s])
        return is_north, far_n, far_s, dst

    def make(t, tile):
        is_north, far_n, far_s, dst = ends(t)
        first = 2 * entries + 3
        src = jnp.where(is_north, far_n, blocks + far_s)
        cls_src = jnp.where(is_north, info_n[first + far_n], info_s[first + far_s])
        build_tile(pos_two, src, pos, dst, cls_src, info[first + dst], amp, scale, tile)

    def use(items):
        terms = []
        for t, tile in items:
            is_north, far_n, far_s, dst = ends(t)
            src = jnp.where(is_north, far_n, blocks + far_s)
            to = jnp.where(t < count, dst, blocks)
            terms.append((to, product(stacked[src], tile[0], tile[1], 0)))
        add_all(acc, terms)

    before = info[2 * entries + 2] + local_pairs
    if build:
        build_loop(before, count, tiles, slots, sems, make, use)
    else:
        read_loop(before, count, tiles, slots, sems, use)

    parts[...] = jnp.zeros_like(parts)
    half = parts.shape[2]

    def finish(b, carry):
        weight = sigma[pl.ds(b, 1), :]
        direction = direct[b]
        result = weight * acc[b] + obs_var[pl.ds(b, 1), :] * direction
        image_out[b] = result
        if build:
            scaled_out[b] = weight * result
        terms = [direction * result]
        if build:
            terms += [direction * direction, result * result]
        for k, term in enumerate(terms):
            parts[k] += term[:, :half] + term[:, half:]
        return carry

    lax.fori_loop(0, blocks, finish, 0)
    if build:
        sums[...] = jnp.zeros_like(sums)
    else:
        sums[...] = sums_in[...]
    for k in range(3 if build else 1):
        row = k if build else 3
        sums[row : row + 1, :] = jnp.sum(jnp.transpose(parts[k]), axis=0, keepdims=True)


def total_kernel(low, high, value, out, held_low, held_high, send_low, recv_low, send_high, recv_high):
    me = lax.axis_index("reg")
    place_low, place_high = lax.rem(me, low), lax.div(me, low)

    def peer(stage, k):
        if stage == 0:
            return me - place_low + lax.rem(place_low + k, low)
        return lax.rem(place_high + k, high) * low + place_low

    barrier = pltpu.get_barrier_semaphore()
    for stage, size in enumerate((low, high)):
        for k in range(1, size):
            pl.semaphore_signal(
                barrier, inc=1, device_id={"reg": peer(stage, k)}, device_id_type=MESH
            )
    pl.semaphore_wait(barrier, low + high - 2)
    running = value[...]
    for stage, size, place, held, send, recv in (
        (0, low, place_low, held_low, send_low, recv_low),
        (1, high, place_high, held_high, send_high, recv_high),
    ):
        held[0] = running
        copies = []
        for k in range(1, size):
            copy = pltpu.make_async_remote_copy(
                src_ref=held.at[0],
                dst_ref=held.at[k],
                send_sem=send.at[k],
                recv_sem=recv.at[k],
                device_id={"reg": peer(stage, k)},
                device_id_type=MESH,
            )
            copy.start()
            copies.append(copy)
        for copy in copies:
            copy.wait()
        running = held[lax.rem(place, size)]
        for source in range(1, size):
            running = running + held[lax.rem(place - source + size, size)]
    out[...] = running


def total_over(value):
    n = lax.axis_size("reg")
    if n & (n - 1) or n < 4:
        return lax.psum(value, "reg")
    low = 1 << ((n.bit_length() - 1) // 2)
    high = n // low
    semaphores = [
        pltpu.SemaphoreType.DMA((size,)) for size in (low, low, high, high)
    ]
    return pl.pallas_call(
        functools.partial(total_kernel, low, high),
        out_shape=jax.ShapeDtypeStruct(value.shape, value.dtype),
        in_specs=[VMEM],
        out_specs=VMEM,
        scratch_shapes=[
            pltpu.VMEM((low,) + value.shape, value.dtype),
            pltpu.VMEM((high,) + value.shape, value.dtype),
        ]
        + semaphores,
        compiler_params=pltpu.CompilerParams(collective_id=0, has_side_effects=True),
        name="member_sums",
    )(value)


def local(
    obs_value,
    positions,
    sigma,
    obs_var,
    class_amp,
    length_scale,
    block_class,
    block_count,
    pair_list,
    pair_count,
):
    blocks, members, size = obs_value.shape
    entries = pair_list.shape[1]
    info = jnp.concatenate(
        [pair_list[0], pair_list[1], pair_count[:, 0], block_count, block_class]
    )
    width = info.shape[0]
    info_rows = -(-width // size)
    packed = jnp.concatenate(
        [
            positions.reshape(2 * blocks, size),
            jnp.pad(info.astype(jnp.float32), (0, -width % size)).reshape(-1, size),
        ]
    )
    packed = jnp.pad(packed, ((0, -packed.shape[0] % members), (0, 0)))
    packed = packed.reshape(-1, members, size)
    scales = jnp.stack([length_scale, 1.0 / length_scale])

    live = (jnp.arange(blocks, dtype=jnp.int32) < block_count[0]).astype(jnp.float32)
    first_residual = obs_value * live[:, None, None]
    scaled = jnp.concatenate([sigma[:, None, :] * first_residual, packed])
    scaled_n = passed_along(scaled, "reg", -1)
    scaled_s = passed_along(scaled, "reg", 1)

    def unpacked(bundle):
        rows = bundle[blocks:].reshape(-1, size)
        listed = rows[2 * blocks : 2 * blocks + info_rows].reshape(-1)[:width]
        return rows[: 2 * blocks].reshape(2, blocks, size), listed.astype(jnp.int32)

    pos_n, info_n = unpacked(scaled_n)
    pos_s, info_s = unpacked(scaled_s)
    pos_two = jnp.concatenate([pos_n, pos_s], axis=1)

    own_cap = blocks + min(SIDE_MAX, entries)
    cross_cap = 2 * min(SIDE_MAX, entries)
    cap = blocks + entries + min(SIDE_MAX, entries) + GROUP - 1
    array = jax.ShapeDtypeStruct((blocks, members, size), jnp.float32)
    spread_shape = jax.ShapeDtypeStruct((blocks + 1, members, size), jnp.float32)
    sums_shape = jax.ShapeDtypeStruct((8, members), jnp.float32)
    tiles_shape = jax.ShapeDtypeStruct((cap, 2, size, size), jnp.bfloat16)

    def scratch(count, build):
        held = (SLOTS,) if build else (2, GROUP)
        return [
            pltpu.VMEM((count, 2 * members, size), jnp.bfloat16),
            pltpu.VMEM(held + (2, size, size), jnp.bfloat16),
            pltpu.SemaphoreType.DMA((SLOTS if build else 2,)),
        ]

    parts = [
        pltpu.VMEM(spread_shape.shape, jnp.float32),
        pltpu.VMEM((3, members, size // 2), jnp.float32),
    ]
    params = pltpu.CompilerParams(vmem_limit_bytes=VMEM_BYTES)

    def cost(count, build):
        return pl.CostEstimate(
            flops=count * 6 * size * size * members + build * count * 80 * size * size,
            bytes_accessed=count * 4 * size * size,
            transcendentals=build * count * size * size,
        )

    tiles, spread = pl.pallas_call(
        functools.partial(own_kernel, True, entries),
        out_shape=[tiles_shape, spread_shape],
        in_specs=[SMEM, SMEM, SMEM, VMEM, VMEM],
        out_specs=[ANY, VMEM],
        scratch_shapes=scratch(blocks, True),
        compiler_params=params,
        cost_estimate=cost(own_cap, 1),
        name="own_tiles_and_spread",
    )(info, class_amp, scales, positions, scaled)
    tiles, image, scaled_image, sums = pl.pallas_call(
        functools.partial(cross_kernel, True, entries),
        out_shape=[tiles_shape, array, array, sums_shape],
        in_specs=[SMEM] * 5 + [VMEM] * 8 + [ANY],
        out_specs=[ANY, VMEM, VMEM, VMEM],
        input_output_aliases={13: 0},
        scratch_shapes=scratch(2 * blocks, True) + parts,
        compiler_params=params,
        cost_estimate=cost(cross_cap, 1),
        name="cross_tiles_and_image",
    )(
        info, info_n, info_s, class_amp, scales, positions, pos_two, scaled_n, scaled_s, spread,
        sigma, obs_var, first_residual, tiles,
    )
    image_n = passed_along(scaled_image, "reg", -1)
    image_s = passed_along(scaled_image, "reg", 1)
    spread = pl.pallas_call(
        functools.partial(own_kernel, False, entries),
        out_shape=spread_shape,
        in_specs=[SMEM, VMEM, ANY],
        out_specs=VMEM,
        scratch_shapes=scratch(blocks, False),
        compiler_params=params,
        cost_estimate=cost(own_cap, 0),
        name="own_spread",
    )(info, scaled_image, tiles)
    second_image, sums = pl.pallas_call(
        functools.partial(cross_kernel, False, entries),
        out_shape=[array, sums_shape],
        in_specs=[SMEM] * 3 + [VMEM] * 7 + [ANY],
        out_specs=[VMEM, VMEM],
        scratch_shapes=scratch(2 * blocks, False) + parts,
        compiler_params=params,
        cost_estimate=cost(cross_cap, 0),
        name="cross_image",
    )(info, info_n, info_s, image_n, image_s, spread, sigma, obs_var, image, sums, tiles)

    totals = total_over(sums)
    curvature, norm = totals[0], totals[1]
    step = norm / curvature
    norm_next = jnp.maximum(norm - 2.0 * step * curvature + step * step * totals[2], 0.0)
    keep = 1.0 + norm_next / norm
    curvature_next = keep * (keep * curvature - 2.0 * step * totals[2]) + step * step * totals[3]
    step_next = norm_next / curvature_next

    def along(member_values):
        return member_values[None, :, None]

    weights = along(step + step_next * keep) * first_residual - along(step_next * step) * image
    residual = (
        first_residual
        - along(step + step_next * keep) * image
        + along(step_next * step) * second_image
    )
    return (weights, residual)


def solution(mesh):
    placed = (
        P(("grp", "reg"), None, None),
        P(None, ("grp", "reg"), None),
        P(("grp", "reg"), None),
        P(("grp", "reg"), None),
        P(),
        P(),
        P(("grp", "reg")),
        P(("grp", "reg")),
        P(None, ("grp", "reg")),
        P(None, ("grp", "reg")),
    )
    return jax.shard_map(
        local,
        mesh=mesh,
        in_specs=placed,
        out_specs=(P(("grp", "reg"), None, None), P(("grp", "reg"), None, None)),
        check_vma=False,
    )
```

time: 255 us -> 203 us (0.80)
  the two profiles are of different devices: /device:TPU:6 before, /device:TPU:0 now
where the time goes in v2:
time: 203 us
  Pallas kernels  111 us (55%)
  starting transfers between devices  48 us (24%)
  waiting for transfers between devices  26.7 us (13%)
  other arithmetic  13.9 us (7%)
  local copies, waits for them, and re-layouts  2.85 us (1%)
    pallas_call x1, Pallas kernels, total_over(): pl.pallas_call(functools.partial(total_kernel, low, high), out_shape=jax....  52.1 us
    ppermute x4, starting transfers between devices, passed_along(): return lax.ppermute(shard, axis, pairs)  48 us
    ppermute x4, waiting for transfers between devices, passed_along(): return lax.ppermute(shard, axis, pairs)  26.7 us
    pallas_call x1, Pallas kernels, local(): pl.pallas_call(functools.partial(own_kernel, True, entries), out_shape=[t...  21.5 us
    pallas_call x1, Pallas kernels, local(): pl.pallas_call(functools.partial(cross_kernel, True, entries), out_shape=...  18.3 us
    pallas_call x1, Pallas kernels, local(): pl.pallas_call(functools.partial(cross_kernel, False, entries), out_shape...  9.48 us
    pallas_call x1, Pallas kernels, local(): pl.pallas_call(functools.partial(own_kernel, False, entries), out_shape=s...  9.13 us
    add x1, other arithmetic, local(): first_residual - along(step + step_next * keep) * image  5.08 us
  transfers between devices with their start and end apart: 4, of which 1 were waited for; matrix products, arithmetic and copies ran while one was open for 0% of the time, Pallas kernels for 15%

profile of v2, /device:TPU:0, one launch (start us, length us, event | category | flops | bytes accessed | tf_op | source)
XLA Modules:
  0.0 203.3 jit_solution(10640054050268492793)
XLA Ops:
  1.3 0.8 slice_bitcast_fusion
  2.0 0.7 concatenate.12.refs_0_
  2.8 0.0 copy-start.6
  2.8 0.8 fusion
  3.6 3.3 %broadcast_multiply_fusion.1 = (f32[16,128,256]{2,1,0:T(8,128)S(1)}, f32[16,128,256]{2,1,0:T(8,128)}) fusion(f32[16,256]{1,0:T(8,128)} %refs_6_.1, f32[16,128,256]{2,1,0:T(8,128)} %param.10, f32[16]{0:T(128)S(1)} %compare_convert_fusion), kind=kLoop, calls=%fused_computation.4 | loop fusion | flops 1048576 | bytes 6307904 | tf_op jit(solution)/shard_map/mul | solution.py:376
  6.9 0.0 copy-done.6
  6.9 0.0 copy-start.7
  6.9 0.1 pad_maximum_fusion.refs_4_
  7.1 0.0 copy-start.3
  7.1 2.5 %collective-permute-start.1 = (f32[17,128,256]{2,1,0:T(8,128)S(1)}, f32[17,128,256]{2,1,0:T(8,128)S(1)}, u32[]{:S(2)}, u32[]{:S(2)}) collective-permute-start(f32[17,128,256]{2,1,0:T(8,128)S(1)} %pad_maximum_fusion.refs_4_), channel_id=1, source_target_pairs={{0,1},{1,2},{2,3},{3,4},{4,5},{5,6},{6,7},{7,8},{8,9},{9,10},{10,1... | collective-permute-start | bytes 6684680 | tf_op jit(solution)/shard_map/ppermute | solution.py:24
  9.6 1.3 collective-permute-start
  10.9 0.0 copy-done.7
  10.9 0.6 pad_maximum_fusion.2.refs_2_.refs_4_
  11.5 0.0 copy-done.3
  11.5 21.5 %own_tiles_and_spread.1 = (bf16[126,2,256,256]{3,2,1,0:T(8,128)(2,1)}, f32[17,128,256]{2,1,0:T(8,128)}) custom-call(s32[141]{0:T(256)} %copy-done.6, f32[3,3]{1,0:T(4,128)} %refs_3_.3, f32[2,3]{1,0:T(2,128)} %pad_maximum_fusion.2.refs_2_.refs_4_, f32[2,16,256]{2,1,0:T(8,128)} %refs_5_.1, f32[17,128,256]{2,1,0:T(8,128)} %copy-done.3), custom_call_target="tpu_custom_call" | custom-call | flops 3445620736 | bytes 16252928 | tf_op jit(solution)/shard_map/own_tiles_and_spread/pallas_call | solution.py:418
  33.0 0.0 collective-permute-done.1.refs_8_
  33.0 0.0 copy-start.1
  33.0 0.0 collective-permute-done.refs_7_
  33.1 0.0 copy-start.2
  33.1 0.7 pad_maximum_fusion.1.refs_6_
  33.8 1.0 slice_convert_fusion
  34.8 0.6 slice_convert_fusion.1
  35.4 0.0 copy-done.1
  35.4 0.0 copy-done.2
  35.4 18.3 %cross_tiles_and_image.1 = (bf16[126,2,256,256]{3,2,1,0:T(8,128)(2,1)}, f32[16,128,256]{2,1,0:T(8,128)}, f32[16,128,256]{2,1,0:T(8,128)}, f32[8,128]{1,0:T(8,128)}) custom-call(s32[141]{0:T(256)} %copy-done.6, s32[141]{0:T(256)} %bitcast.66, s32[141]{0:T(256)} %bitcast.64, f32[3,3]{1,0:T(4,128)} %refs_3_.3, ...), custom_call_target="tpu_custom_call", output_to_operand_aliasing={{0}: (13, {})} | custom-call | flops 5112856576 | bytes 24117248 | tf_op jit(solution)/shard_map/cross_tiles_and_image/pallas_call | solution.py:428
  53.7 42.9 %collective-permute-start.3 = (f32[16,128,256]{2,1,0:T(8,128)}, f32[16,128,256]{2,1,0:T(8,128)S(1)}, u32[]{:S(2)}, u32[]{:S(2)}) collective-permute-start(f32[16,128,256]{2,1,0:T(8,128)} %get-tuple-element.12.refs_1_), channel_id=1, source_target_pairs={{0,1},{1,2},{2,3},{3,4},{4,5},{5,6},{6,7},{7,8},{8,9},{9,10},{10,1... | collective-permute-start | bytes 6291464 | tf_op jit(solution)/shard_map/ppermute | solution.py:24
  96.6 1.3 collective-permute-start.2
  97.9 9.1 %own_spread.1.refs_5_ = f32[17,128,256]{2,1,0:T(8,128)} custom-call(s32[141]{0:T(256)} %copy-done.6, f32[16,128,256]{2,1,0:T(8,128)} %get-tuple-element.12.refs_1_, bf16[126,2,256,256]{3,2,1,0:T(8,128)(2,1)} %get-tuple-element.13.refs_2_.refs_10_), custom_call_target="tpu_custom_call" | custom-call | flops 3120562176 | bytes 16252928 | tf_op jit(solution)/shard_map/own_spread/pallas_call | solution.py:444
  107.0 0.0 collective-permute-done.3.refs_4_
  107.0 0.0 copy-start.4
  107.1 26.6 %collective-permute-done.2.refs_3_ = f32[16,128,256]{2,1,0:T(8,128)S(1)} collective-permute-done((f32[16,128,256]{2,1,0:T(8,128)}, f32[16,128,256]{2,1,0:T(8,128)S(1)}, u32[]{:S(2)}, u32[]{:S(2)}) %collective-permute-start.2) | collective-permute-done | bytes 2097184 | tf_op jit(solution)/shard_map/ppermute | solution.py:24
  133.7 0.0 copy-start.5
  133.7 0.0 copy-done.4
  133.7 1.3 copy-done.5
  135.0 0.0 copy-start
  135.0 9.5 %cross_image.1 = (f32[16,128,256]{2,1,0:T(8,128)}, f32[8,128]{1,0:T(8,128)}) custom-call(s32[141]{0:T(256)} %copy-done.6, s32[141]{0:T(256)} %bitcast.67, s32[141]{0:T(256)} %bitcast.65, f32[16,128,256]{2,1,0:T(8,128)} %copy-done.5, f32[16,128,256]{2,1,0:T(8,128)} %copy-done.4, f32[17,128,256]{2,1,0:T(8,128)} %own_spread.1.refs_5_, f32[16,256]{1,0:T(8,128)} %refs_6_.1, ...), custom_call_target="tpu_custom_call" | custom-call | flops 4630511616 | bytes 24117248 | tf_op jit(solution)/shard_map/cross_image/pallas_call | solution.py:454
  144.5 52.1 %member_sums.1 = f32[8,128]{1,0:T(8,128)} custom-call(f32[8,128]{1,0:T(8,128)} %get-tuple-element.16.value), custom_call_target="tpu_custom_call" | custom-call | tf_op jit(solution)/shard_map/member_sums/pallas_call | solution.py:330
  196.6 0.8 fusion.8
  197.4 0.8 multiply_add_fusion.1
  198.2 0.0 copy-done
  198.3 5.1 %multiply_add_fusion = (f32[16,128,256]{2,1,0:T(8,128)}, f32[16,128,256]{2,1,0:T(8,128)}) fusion(f32[16,128,256]{2,1,0:T(8,128)} %get-tuple-element.17, f32[16,128,256]{2,1,0:T(8,128)S(1)} %copy-done, f32[16,128,256]{2,1,0:T(8,128)} %get-tuple-element.14.refs_8_, f32[128]{0:T(128)S(1)} %mul.157, f32[128]{0:T(128)S(1)} %get-tuple-element.18), kind=kLoop, calls=%fused_computation.1 | loop fusion | flops 3670016 | bytes 10486784 | tf_op jit(solution)/shard_map/add | solution.py:478
  (7 shorter events, 0.0 us)
Async XLA Ops:
  2.8 4.1 %copy-start.6 = (s32[141]{0:T(256)}, s32[141]{0:T(256)S(1)}, u32[]{:S(2)}) copy-start(s32[141]{0:T(256)S(1)} %concatenate.12.refs_0_) | copy-start | bytes 1696
  6.9 4.0 %copy-start.7 = (f32[3]{0:T(128)S(1)}, f32[3]{0:T(128)}, u32[]{:S(2)}) copy-start(f32[3]{0:T(128)} %param.15) | copy-start | bytes 40
  7.1 4.4 %copy-start.3 = (f32[17,128,256]{2,1,0:T(8,128)}, f32[17,128,256]{2,1,0:T(8,128)S(1)}, u32[]{:S(2)}) copy-start(f32[17,128,256]{2,1,0:T(8,128)S(1)} %pad_maximum_fusion.refs_4_) | copy-start | bytes 6684676
  7.1 25.9 %collective-permute-start.1 = (f32[17,128,256]{2,1,0:T(8,128)S(1)}, f32[17,128,256]{2,1,0:T(8,128)S(1)}, u32[]{:S(2)}, u32[]{:S(2)}) collective-permute-start(f32[17,128,256]{2,1,0:T(8,128)S(1)} %pad_maximum_fusion.refs_4_), channel_id=1, source_target_pairs={{0,1},{1,2},{2,3},{3,4},{4,5},{5,6},{6,7},{7,8},{8,9},{9,10},{10,1... | collective-permute-start | bytes 6684680 | tf_op jit(solution)/shard_map/ppermute | solution.py:24
  9.6 23.5 %collective-permute-start = (f32[17,128,256]{2,1,0:T(8,128)S(1)}, f32[17,128,256]{2,1,0:T(8,128)S(1)}, u32[]{:S(2)}, u32[]{:S(2)}) collective-permute-start(f32[17,128,256]{2,1,0:T(8,128)S(1)} %pad_maximum_fusion.refs_4_), channel_id=1, source_target_pairs={{1,0},{2,1},{3,2},{4,3},{5,4},{6,5},{7,6},{8,7},{9,8},{10,9},{11,1... | collective-permute-start | bytes 6684680 | tf_op jit(solution)/shard_map/ppermute | solution.py:24
  33.0 2.4 %copy-start.1 = (f32[17,128,256]{2,1,0:T(8,128)}, f32[17,128,256]{2,1,0:T(8,128)S(1)}, u32[]{:S(2)}) copy-start(f32[17,128,256]{2,1,0:T(8,128)S(1)} %collective-permute-done.1.refs_8_) | copy-start | bytes 6684676
  33.1 2.3 %copy-start.2 = (f32[17,128,256]{2,1,0:T(8,128)}, f32[17,128,256]{2,1,0:T(8,128)S(1)}, u32[]{:S(2)}) copy-start(f32[17,128,256]{2,1,0:T(8,128)S(1)} %collective-permute-done.refs_7_) | copy-start | bytes 6684676
  53.7 53.3 %collective-permute-start.3 = (f32[16,128,256]{2,1,0:T(8,128)}, f32[16,128,256]{2,1,0:T(8,128)S(1)}, u32[]{:S(2)}, u32[]{:S(2)}) collective-permute-start(f32[16,128,256]{2,1,0:T(8,128)} %get-tuple-element.12.refs_1_), channel_id=1, source_target_pairs={{0,1},{1,2},{2,3},{3,4},{4,5},{5,6},{6,7},{7,8},{8,9},{9,10},{10,1... | collective-permute-start | bytes 6291464 | tf_op jit(solution)/shard_map/ppermute | solution.py:24
  96.6 37.1 %collective-permute-start.2 = (f32[16,128,256]{2,1,0:T(8,128)}, f32[16,128,256]{2,1,0:T(8,128)S(1)}, u32[]{:S(2)}, u32[]{:S(2)}) collective-permute-start(f32[16,128,256]{2,1,0:T(8,128)} %get-tuple-element.12.refs_1_), channel_id=1, source_target_pairs={{1,0},{2,1},{3,2},{4,3},{5,4},{6,5},{7,6},{8,7},{9,8},{10,9},{11,1... | collective-permute-start | bytes 6291464 | tf_op jit(solution)/shard_map/ppermute | solution.py:24
  107.0 26.7 %copy-start.4 = (f32[16,128,256]{2,1,0:T(8,128)}, f32[16,128,256]{2,1,0:T(8,128)S(1)}, u32[]{:S(2)}) copy-start(f32[16,128,256]{2,1,0:T(8,128)S(1)} %collective-permute-done.3.refs_4_) | copy-start | bytes 6291460
  133.7 1.3 copy-start.5
  135.0 63.2 %copy-start = (f32[16,128,256]{2,1,0:T(8,128)S(1)}, f32[16,128,256]{2,1,0:T(8,128)}, u32[]{:S(2)}) copy-start(f32[16,128,256]{2,1,0:T(8,128)} %get-tuple-element.24.refs_12_) | copy-start | bytes 6291460
